TPU v7x, 32 devices: a whole 2x2x4 slice. The times are simulated.
32 devices in a mesh: row: 4 (over y, core), col: 8 (over z, x).
Axes of the slice: x: 2, y: 2, z: 4, core: 2. Of those that a mesh axis runs over, the one named last changes fastest.
Arguments:
- slab_points: bfloat16 [64, 4096], P(None, ('row', 'col')), may hold values from -6 to 6
- col_points: bfloat16 [64, 131072], P(None, 'col'), may hold values from -6 to 6
- probes: bfloat16 [64, 131072], P(None, 'col'), may hold values from -6 to 6
Outputs:
- basis: bfloat16 [64, 4096], P(None, ('row', 'col'))
- image: float32 [64, 131072], P(None, ('col', 'row'))
All inputs are finite; a program needn't handle non-finite values.
Results may differ from a plain program's by a relative error of at most 0.0052.
Values may be sent and summed in bfloat16 or wider, within the bound.
No kernel may reach another device: no remote copies, remote signals or barrier semaphores. Data moves between devices by JAX's collectives and lax.ppermute only.
A program may use at most 128 MiB of HBM per device.

v0:
```python
import math

import jax
import jax.numpy as jnp
from jax import lax
from jax.sharding import PartitionSpec as P


def body(slab_points, col_points, probes):
    slab_whole = lax.all_gather(slab_points, "col", axis=1, tiled=True)
    dims = slab_whole.shape[0]
    slab_count = slab_whole.shape[1]
    col_count = col_points.shape[1]
    width = math.gcd(col_count, 2048)
    blocks = col_count // width
    slab_total = slab_count * lax.axis_size("row")
    point_total = col_count * lax.axis_size("col")
    share = slab_count // lax.axis_size("col")
    slab_norm = jnp.sum(slab_whole.astype(jnp.float32) ** 2, axis=0)
    col_norm = jnp.sum(col_points.astype(jnp.float32) ** 2, axis=0)

    def make_tile(start):
        cols = lax.dynamic_slice_in_dim(col_points, start, width, 1)
        norms = lax.dynamic_slice_in_dim(col_norm, start, width, 0)
        inner = lax.dot_general(
            slab_whole, cols, (((0,), (0,)), ((), ())), preferred_element_type=jnp.float32
        )
        distance = slab_norm[:, None] + norms[None, :] - 2.0 * inner
        return jnp.exp(-8.0 * distance / dims).astype(jnp.bfloat16)

    def sample_step(total, which):
        start = which * width
        kernel = make_tile(start)
        probe_block = lax.dynamic_slice_in_dim(probes, start, width, 1)
        total = total + lax.dot_general(
            probe_block, kernel, (((1,), (1,)), ((), ())), preferred_element_type=jnp.float32
        )
        return (total, None)

    empty = jnp.zeros((probes.shape[0], slab_count), jnp.float32)
    partial_value, stored = lax.scan(sample_step, empty, jnp.arange(blocks, dtype=jnp.int32))
    sample = lax.psum(partial_value, "col")
    gram = lax.psum(jnp.dot(sample, sample.T, precision=lax.Precision.HIGHEST), "row") / slab_total
    lower = jnp.linalg.cholesky(gram)
    basis_full = jax.scipy.linalg.solve_triangular(lower, sample, lower=True).astype(jnp.bfloat16)
    basis_own = lax.dynamic_slice_in_dim(basis_full, lax.axis_index("col") * share, share, 1)

    def image_step(which, result):
        start = which * width
        kernel = make_tile(start)
        block_out = jnp.dot(basis_full, kernel, preferred_element_type=jnp.float32)
        return lax.dynamic_update_slice_in_dim(result, block_out, start, 1)

    terms = lax.fori_loop(
        0, blocks, image_step, jnp.zeros((probes.shape[0], col_count), jnp.float32)
    )
    image_scale = (
        jnp.sqrt(jnp.float32(probes.shape[0] * point_total) / jnp.trace(gram)) / slab_total
    )
    image = lax.psum_scatter(terms, "row", scatter_dimension=1, tiled=True) * image_scale
    return (basis_own, image)


def solution(mesh):
    return jax.shard_map(
        body,
        mesh=mesh,
        in_specs=(P(None, ("row", "col")), P(None, "col"), P(None, "col")),
        out_specs=(P(None, ("row", "col")), P(None, ("col", "row"))),
        check_vma=False,
    )
```

profile of v0, /device:TPU:0, one launch (start us, length us, event | category | flops | bytes accessed | tf_op | source)
XLA Modules:
  0.0 267.4 jit_solution(5741968966510597757)
XLA Ops:
  7.2 0.0 all-reduce.2.cloned.1.call-start
  7.2 28.1 %all_gather.3 = bf16[64,1024]{1,0:T(8,128)(2,1)S(1)} all-gather(bf16[64,128]{1,0:T(8,128)(2,1)} %param.7), channel_id=1, replica_groups=mesh['row'=4,'col'=8] {'col'}, dimensions={1}, use_global_device_ids=true | all-gather | bytes 147456 | tf_op jit(solution)/shard_map/all_gather | solution.py:10
  35.4 2.1 multiply_reduce_fusion
  37.5 42.7 %while.29 = (s32[]{:T(128)}, f32[64,1024]{1,0:T(8,128)S(1)}, s32[8]{0:T(128)S(1)}, bf16[64,16384]{1,0:T(8,128)(2,1)}, f32[1024]{0:T(1024)S(1)}, /*index=5*/f32[1...) while((s32[]{:T(128)}, f32[64,1024]{1,0:T(8,128)S(1)}, ...), condition=%wide.region_3.4_spmd.clone, body=%wide.region_2.3_spmd.clone.sunk | while | flops 547487744 | bytes 1210044 | solution.py:41
  37.5 0.6 dynamic_slice.72
  38.8 4.1 %fusion.47 = f32[64,1024]{1,0:T(8,128)S(1)} fusion(bf16[64,1024]{1,0:T(8,128)(2,1)S(1)} %get-tuple-element.463, f32[2048]{0:T(1024)S(1)} %dynamic_slice.73, f32[1024]{0:T(1024)S(1)} %get-tuple-element.460, f32[64,1024]{1,0:T(8,128)S(1)} %get-tuple-element.445, bf16[64,16384]{1,0:T(8,128)(2,1)} %get-tuple-element.462, s32[]{:T(128)S(6)} %select_n.43, ...), kind=kOutput, calls=%fused_computation.15.clone.1 | convolution fusion | flops 547487744 | bytes 1193472 | tf_op jit(solution)/shard_map/while/body/eval_jaxpr/dot_general | solution.py:35
  42.9 0.6 dynamic_slice.72
  44.1 4.0 %fusion.47 = f32[64,1024]{1,0:T(8,128)S(1)} fusion(bf16[64,1024]{1,0:T(8,128)(2,1)S(1)} %get-tuple-element.463, f32[2048]{0:T(1024)S(1)} %dynamic_slice.73, f32[1024]{0:T(1024)S(1)} %get-tuple-element.460, f32[64,1024]{1,0:T(8,128)S(1)} %get-tuple-element.445, bf16[64,16384]{1,0:T(8,128)(2,1)} %get-tuple-element.462, s32[]{:T(128)S(6)} %select_n.43, ...), kind=kOutput, calls=%fused_computation.15.clone.1 | convolution fusion | flops 547487744 | bytes 1193472 | tf_op jit(solution)/shard_map/while/body/eval_jaxpr/dot_general | solution.py:35
  48.2 0.6 dynamic_slice.72
  49.5 4.0 %fusion.47 = f32[64,1024]{1,0:T(8,128)S(1)} fusion(bf16[64,1024]{1,0:T(8,128)(2,1)S(1)} %get-tuple-element.463, f32[2048]{0:T(1024)S(1)} %dynamic_slice.73, f32[1024]{0:T(1024)S(1)} %get-tuple-element.460, f32[64,1024]{1,0:T(8,128)S(1)} %get-tuple-element.445, bf16[64,16384]{1,0:T(8,128)(2,1)} %get-tuple-element.462, s32[]{:T(128)S(6)} %select_n.43, ...), kind=kOutput, calls=%fused_computation.15.clone.1 | convolution fusion | flops 547487744 | bytes 1193472 | tf_op jit(solution)/shard_map/while/body/eval_jaxpr/dot_general | solution.py:35
  53.5 0.6 dynamic_slice.72
  54.8 4.0 %fusion.47 = f32[64,1024]{1,0:T(8,128)S(1)} fusion(bf16[64,1024]{1,0:T(8,128)(2,1)S(1)} %get-tuple-element.463, f32[2048]{0:T(1024)S(1)} %dynamic_slice.73, f32[1024]{0:T(1024)S(1)} %get-tuple-element.460, f32[64,1024]{1,0:T(8,128)S(1)} %get-tuple-element.445, bf16[64,16384]{1,0:T(8,128)(2,1)} %get-tuple-element.462, s32[]{:T(128)S(6)} %select_n.43, ...), kind=kOutput, calls=%fused_computation.15.clone.1 | convolution fusion | flops 547487744 | bytes 1193472 | tf_op jit(solution)/shard_map/while/body/eval_jaxpr/dot_general | solution.py:35
  58.9 0.6 dynamic_slice.72
  60.1 4.0 %fusion.47 = f32[64,1024]{1,0:T(8,128)S(1)} fusion(bf16[64,1024]{1,0:T(8,128)(2,1)S(1)} %get-tuple-element.463, f32[2048]{0:T(1024)S(1)} %dynamic_slice.73, f32[1024]{0:T(1024)S(1)} %get-tuple-element.460, f32[64,1024]{1,0:T(8,128)S(1)} %get-tuple-element.445, bf16[64,16384]{1,0:T(8,128)(2,1)} %get-tuple-element.462, s32[]{:T(128)S(6)} %select_n.43, ...), kind=kOutput, calls=%fused_computation.15.clone.1 | convolution fusion | flops 547487744 | bytes 1193472 | tf_op jit(solution)/shard_map/while/body/eval_jaxpr/dot_general | solution.py:35
  64.2 0.6 dynamic_slice.72
  65.4 4.0 %fusion.47 = f32[64,1024]{1,0:T(8,128)S(1)} fusion(bf16[64,1024]{1,0:T(8,128)(2,1)S(1)} %get-tuple-element.463, f32[2048]{0:T(1024)S(1)} %dynamic_slice.73, f32[1024]{0:T(1024)S(1)} %get-tuple-element.460, f32[64,1024]{1,0:T(8,128)S(1)} %get-tuple-element.445, bf16[64,16384]{1,0:T(8,128)(2,1)} %get-tuple-element.462, s32[]{:T(128)S(6)} %select_n.43, ...), kind=kOutput, calls=%fused_computation.15.clone.1 | convolution fusion | flops 547487744 | bytes 1193472 | tf_op jit(solution)/shard_map/while/body/eval_jaxpr/dot_general | solution.py:35
  69.5 0.6 dynamic_slice.72
  70.8 4.0 %fusion.47 = f32[64,1024]{1,0:T(8,128)S(1)} fusion(bf16[64,1024]{1,0:T(8,128)(2,1)S(1)} %get-tuple-element.463, f32[2048]{0:T(1024)S(1)} %dynamic_slice.73, f32[1024]{0:T(1024)S(1)} %get-tuple-element.460, f32[64,1024]{1,0:T(8,128)S(1)} %get-tuple-element.445, bf16[64,16384]{1,0:T(8,128)(2,1)} %get-tuple-element.462, s32[]{:T(128)S(6)} %select_n.43, ...), kind=kOutput, calls=%fused_computation.15.clone.1 | convolution fusion | flops 547487744 | bytes 1193472 | tf_op jit(solution)/shard_map/while/body/eval_jaxpr/dot_general | solution.py:35
  74.8 0.6 dynamic_slice.72
  76.1 4.0 %fusion.47 = f32[64,1024]{1,0:T(8,128)S(1)} fusion(bf16[64,1024]{1,0:T(8,128)(2,1)S(1)} %get-tuple-element.463, f32[2048]{0:T(1024)S(1)} %dynamic_slice.73, f32[1024]{0:T(1024)S(1)} %get-tuple-element.460, f32[64,1024]{1,0:T(8,128)S(1)} %get-tuple-element.445, bf16[64,16384]{1,0:T(8,128)(2,1)} %get-tuple-element.462, s32[]{:T(128)S(6)} %select_n.43, ...), kind=kOutput, calls=%fused_computation.15.clone.1 | convolution fusion | flops 547487744 | bytes 1193472 | tf_op jit(solution)/shard_map/while/body/eval_jaxpr/dot_general | solution.py:35
  80.2 0.0 copy-start
  80.2 0.7 copy-done
  80.9 0.0 all-reduce.2.cloned.1.call-update
  80.9 0.0 reduce-scatter.2.cloned.1.call-start
  80.9 69.9 %all-reduce.2.cloned.1.call-done = f32[64,1024]{1,0:T(8,128)} async-done(((f32[64,1024]{1,0:T(8,128)}), f32[64,1024]{1,0:T(8,128)}) %all-reduce.2.cloned.1.call-update) | async-done | bytes 262160 | tf_op jit(solution)/shard_map/psum | solution.py:42
  150.9 1.4 fusion.25
  152.3 10.3 %psum.15 = f32[64,64]{1,0:T(8,128)S(1)} all-reduce(f32[64,64]{1,0:T(8,128)S(1)} %fusion.25), channel_id=1, replica_groups=mesh['row'=4,'col'=8] {'row'}, use_global_device_ids=true, to_apply=%region_5.6 | all-reduce | flops 4096 | bytes 32768 | tf_op jit(solution)/shard_map/psum | solution.py:43
  162.6 0.1 copy.5
  162.6 0.6 select_reduce_fusion
  163.3 5.8 %cholesky.17 = f32[64,64]{1,0:T(8,128)S(1)} custom-call(f32[64,64]{1,0:T(8,128)S(1)} %get-tuple-element.339), custom_call_target="Cholesky" | custom-call | tf_op jit(solution)/shard_map/jit(cholesky)/cholesky | solution.py:44
  169.1 0.7 compare_reduce_fusion
  169.8 0.6 fusion.22
  170.5 4.9 %custom-call.7 = f32[1,64,64]{1,2,0:T(8,128)S(1)} custom-call(f32[1,64,64]{2,1,0:T(8,128)S(1)} %fusion.22), custom_call_target="InvertDiagBlocksLowerTriangular" | custom-call | tf_op jit(solution)/shard_map/jit(_solve_triangular)/triangular_solve | solution.py:45
  175.4 1.4 convolution_convert_fusion
  176.8 2.3 broadcast_in_dim.19
  179.0 35.2 %while.28 = (s32[]{:T(128)}, f32[64,16384]{1,0:T(8,128)}, f32[1024]{0:T(1024)S(1)}, f32[16384]{0:T(1024)S(1)}, bf16[64,16384]{1,0:T(8,128)(2,1)}, /*index=5*/bf1...) while((s32[]{:T(128)}, f32[64,16384]{1,0:T(8,128)}, ...), condition=%wide.region_9.10_spmd, body=%wide.region_8.9_spmd.sunk | while | flops 547356672 | bytes 1078431 | solution.py:54
  179.0 4.4 %fusion.43 = f32[64,16384]{1,0:T(8,128)} fusion(f32[64,16384]{1,0:T(8,128)} %get-tuple-element.480, s32[]{:T(128)S(6)} %select_n.42, bf16[64,1024]{1,0:T(8,128)(2,1)S(1)} %get-tuple-element.496, bf16[64,1024]{1,0:T(8,128)(2,1)S(1)} %get-tuple-element.495, f32[2048]{0:T(1024)S(1)} %dynamic_slice.69, f32[1024]{0:T(1024)S(1)} %get-tuple-element.492, ...), kind=kOutput, calls=%fused_computation.5.clone.1 | convolution fusion | flops 547356672 | bytes 1061888 | tf_op jit(solution)/shard_map/while/body/eval_jaxpr/dot_general | solution.py:51
  183.4 4.4 %fusion.43 = f32[64,16384]{1,0:T(8,128)} fusion(f32[64,16384]{1,0:T(8,128)} %get-tuple-element.480, s32[]{:T(128)S(6)} %select_n.42, bf16[64,1024]{1,0:T(8,128)(2,1)S(1)} %get-tuple-element.496, bf16[64,1024]{1,0:T(8,128)(2,1)S(1)} %get-tuple-element.495, f32[2048]{0:T(1024)S(1)} %dynamic_slice.69, f32[1024]{0:T(1024)S(1)} %get-tuple-element.492, ...), kind=kOutput, calls=%fused_computation.5.clone.1 | convolution fusion | flops 547356672 | bytes 1061888 | tf_op jit(solution)/shard_map/while/body/eval_jaxpr/dot_general | solution.py:51
  187.8 4.4 %fusion.43 = f32[64,16384]{1,0:T(8,128)} fusion(f32[64,16384]{1,0:T(8,128)} %get-tuple-element.480, s32[]{:T(128)S(6)} %select_n.42, bf16[64,1024]{1,0:T(8,128)(2,1)S(1)} %get-tuple-element.496, bf16[64,1024]{1,0:T(8,128)(2,1)S(1)} %get-tuple-element.495, f32[2048]{0:T(1024)S(1)} %dynamic_slice.69, f32[1024]{0:T(1024)S(1)} %get-tuple-element.492, ...), kind=kOutput, calls=%fused_computation.5.clone.1 | convolution fusion | flops 547356672 | bytes 1061888 | tf_op jit(solution)/shard_map/while/body/eval_jaxpr/dot_general | solution.py:51
  192.2 4.4 %fusion.43 = f32[64,16384]{1,0:T(8,128)} fusion(f32[64,16384]{1,0:T(8,128)} %get-tuple-element.480, s32[]{:T(128)S(6)} %select_n.42, bf16[64,1024]{1,0:T(8,128)(2,1)S(1)} %get-tuple-element.496, bf16[64,1024]{1,0:T(8,128)(2,1)S(1)} %get-tuple-element.495, f32[2048]{0:T(1024)S(1)} %dynamic_slice.69, f32[1024]{0:T(1024)S(1)} %get-tuple-element.492, ...), kind=kOutput, calls=%fused_computation.5.clone.1 | convolution fusion | flops 547356672 | bytes 1061888 | tf_op jit(solution)/shard_map/while/body/eval_jaxpr/dot_general | solution.py:51
  196.6 4.4 %fusion.43 = f32[64,16384]{1,0:T(8,128)} fusion(f32[64,16384]{1,0:T(8,128)} %get-tuple-element.480, s32[]{:T(128)S(6)} %select_n.42, bf16[64,1024]{1,0:T(8,128)(2,1)S(1)} %get-tuple-element.496, bf16[64,1024]{1,0:T(8,128)(2,1)S(1)} %get-tuple-element.495, f32[2048]{0:T(1024)S(1)} %dynamic_slice.69, f32[1024]{0:T(1024)S(1)} %get-tuple-element.492, ...), kind=kOutput, calls=%fused_computation.5.clone.1 | convolution fusion | flops 547356672 | bytes 1061888 | tf_op jit(solution)/shard_map/while/body/eval_jaxpr/dot_general | solution.py:51
  201.0 4.4 %fusion.43 = f32[64,16384]{1,0:T(8,128)} fusion(f32[64,16384]{1,0:T(8,128)} %get-tuple-element.480, s32[]{:T(128)S(6)} %select_n.42, bf16[64,1024]{1,0:T(8,128)(2,1)S(1)} %get-tuple-element.496, bf16[64,1024]{1,0:T(8,128)(2,1)S(1)} %get-tuple-element.495, f32[2048]{0:T(1024)S(1)} %dynamic_slice.69, f32[1024]{0:T(1024)S(1)} %get-tuple-element.492, ...), kind=kOutput, calls=%fused_computation.5.clone.1 | convolution fusion | flops 547356672 | bytes 1061888 | tf_op jit(solution)/shard_map/while/body/eval_jaxpr/dot_general | solution.py:51
  205.4 4.4 %fusion.43 = f32[64,16384]{1,0:T(8,128)} fusion(f32[64,16384]{1,0:T(8,128)} %get-tuple-element.480, s32[]{:T(128)S(6)} %select_n.42, bf16[64,1024]{1,0:T(8,128)(2,1)S(1)} %get-tuple-element.496, bf16[64,1024]{1,0:T(8,128)(2,1)S(1)} %get-tuple-element.495, f32[2048]{0:T(1024)S(1)} %dynamic_slice.69, f32[1024]{0:T(1024)S(1)} %get-tuple-element.492, ...), kind=kOutput, calls=%fused_computation.5.clone.1 | convolution fusion | flops 547356672 | bytes 1061888 | tf_op jit(solution)/shard_map/while/body/eval_jaxpr/dot_general | solution.py:51
  209.8 4.4 %fusion.43 = f32[64,16384]{1,0:T(8,128)} fusion(f32[64,16384]{1,0:T(8,128)} %get-tuple-element.480, s32[]{:T(128)S(6)} %select_n.42, bf16[64,1024]{1,0:T(8,128)(2,1)S(1)} %get-tuple-element.496, bf16[64,1024]{1,0:T(8,128)(2,1)S(1)} %get-tuple-element.495, f32[2048]{0:T(1024)S(1)} %dynamic_slice.69, f32[1024]{0:T(1024)S(1)} %get-tuple-element.492, ...), kind=kOutput, calls=%fused_computation.5.clone.1 | convolution fusion | flops 547356672 | bytes 1061888 | tf_op jit(solution)/shard_map/while/body/eval_jaxpr/dot_general | solution.py:51
  214.2 0.0 reduce-scatter.2.cloned.1.call-update
  214.9 0.6 constant_dynamic-slice_fusion
  215.5 42.7 %reduce-scatter.2.cloned.1.call-done = f32[64,4096]{1,0:T(8,128)} async-done(((f32[64,16384]{1,0:T(8,128)}), f32[64,4096]{1,0:T(8,128)}) %reduce-scatter.2.cloned.1.call-update) | async-done | bytes 1048592 | tf_op jit(solution)/shard_map/reduce_scatter | solution.py:60
  258.3 2.3 broadcast_multiply_fusion
  (21 shorter events, 0.2 us)
Async XLA Ops:
  7.2 143.7 %all-reduce.2.cloned.1.call-start = ((), (), s32[]{:S(2)}) async-start(), calls=%async_computation.1 | async-start | bytes 524288 | tf_op jit(solution)/shard_map/psum | solution.py:42
  80.2 0.7 copy-start
  80.9 177.4 %reduce-scatter.2.cloned.1.call-start = ((), (), s32[]{:S(2)}) async-start(), calls=%async_computation.2 | async-start | bytes 5242880 | tf_op jit(solution)/shard_map/reduce_scatter | solution.py:60
Sparse Core Ops, SparseCore 0:
  81.0 69.8 all-reduce.1
  214.3 43.8 reduce-scatter.1
where the time goes:
time: 268 us; the launch traced here: 267 us
  waiting for transfers between devices  113 us (42%)
  matrix products  70.3 us (26%)
  blocking collectives  38.4 us (14%)
  other arithmetic  17.2 us (6%)
  between operations  14.9 us (6%)
  local copies, waits for them, and re-layouts  8.42 us (3%)
  loops' own time  5.54 us (2%)
    psum x1, waiting for transfers between devices, body(): sample = lax.psum(partial_value, 'col')  69.9 us
    reduce_scatter x1, waiting for transfers between devices, body(): lax.psum_scatter(terms, 'row', scatter_dimension=1, tiled=True)  42.7 us
    dot_general x8, matrix products, image_step(): block_out = jnp.dot(basis_full, kernel, preferred_element_type=jnp.float32)  35.1 us
    dot_general x8, matrix products, sample_step(): lax.dot_general(probe_block, kernel, (((1,), (1,)), ((), ())), preferred_...  32.4 us
    all_gather x1, blocking collectives, body(): slab_whole = lax.all_gather(slab_points, 'col', axis=1, tiled=True)  28.1 us
    psum x1, blocking collectives, body(): lax.psum(jnp.dot(sample, sample.T, precision=lax.Precision.HIGHEST), 'row')  10.3 us
    another operation x3, other arithmetic, body(): lower = jnp.linalg.cholesky(gram)  6.58 us
    another operation x1, loops' own time, body(): lax.scan(sample_step, empty, jnp.arange(blocks, dtype=jnp.int32))  5.54 us
  transfers between devices with their start and end apart: 2, of which 2 were waited for; matrix products, arithmetic and copies ran while one was open for 0% of the time, Pallas kernels for 0%

commit v1 on v0

v1 whole, which is shorter than its diff:
```python
import functools

import jax
import jax.numpy as jnp
from jax import lax
from jax.experimental import pallas as pl
from jax.experimental.pallas import tpu as pltpu
from jax.sharding import PartitionSpec as P

MIB = 1024 * 1024


def params(mib):
    return pltpu.CompilerParams(vmem_limit_bytes=mib * MIB)


def split(x, pieces):
    out = []
    for _ in range(pieces):
        piece = x.astype(jnp.bfloat16)
        x = x - piece.astype(jnp.float32)
        out.append(piece)
    return out


def extended(points, scale=None):
    dims, count = points.shape
    wide = points.astype(jnp.float32)
    norm = -0.5 * jnp.sum(wide * wide, axis=0, keepdims=True)
    row = lax.broadcasted_iota(jnp.int32, (128 - dims, count), 0)
    at = 3 if scale is None else 0
    ones = 3 - at
    factor = 1.0 if scale is None else scale
    extra = jnp.where((row >= ones) & (row < ones + 3), factor, 0.0)
    for i, piece in enumerate(split(norm, 3)):
        extra = jnp.where(row == at + i, piece.astype(jnp.float32) * factor, extra)
    if scale is not None:
        points = (wide * scale).astype(jnp.bfloat16)
    return jnp.concatenate([points, extra.astype(jnp.bfloat16)], axis=0)


def chunks_of(*refs):
    return [ref[i] for ref in refs for i in range(ref.shape[0])]


def resident(shape, dtype):
    return pltpu.VMEM(shape, dtype)


def held(x):
    return pltpu.with_memory_space_constraint(x, pltpu.VMEM)


def pinned(x):
    return pltpu.with_memory_space_constraint(x, pltpu.HBM)


WHOLE = pl.BlockSpec(memory_space=pltpu.VMEM)
SCALAR = pl.BlockSpec(memory_space=pltpu.SMEM)


def add_sample(slab_ext, cols, probes, total, kept_ref, first, mine):
    step = min(256, total.shape[1])
    group = 4096
    size = 512
    own = kept_ref.shape[0] - size
    places = []
    for j in range(cols.shape[0] // size):
        place = first + j * size - mine
        place = jnp.where((place >= 0) & (place < own), place, own)
        places.append(pl.ds(pl.multiple_of(place, size), size))
    for i in range(total.shape[1] // step):
        at = slice(i * step, (i + 1) * step)
        slab = slab_ext[:, at]
        for g in range(cols.shape[0] // group):
            kernel = []
            for j in range(g * group // size, (g + 1) * group // size):
                rows = slice(j * size, (j + 1) * size)
                x = jnp.dot(cols[rows, :], slab, preferred_element_type=jnp.float32)
                k = jnp.exp(x).astype(jnp.bfloat16)
                kept_ref[places[j], at] = k
                kernel.append(k)
            total[:, at] += jnp.dot(
                probes[:, g * group : (g + 1) * group],
                jnp.concatenate(kernel, axis=0),
                preferred_element_type=jnp.float32,
            )


def start_sample(chunks, me_ref, slab_ref, slab_ext, total):
    side = me_ref[0] & 1
    points = [slab_ref[2 * k + (side ^ flip)] for k, flip in chunks]
    slab_ext[...] = extended(jnp.concatenate(points, axis=1), scale_of(slab_ref))
    total[...] = jnp.zeros_like(total)


def scale_of(slab_ref):
    return 16.0 / slab_ref.shape[1]


def end_sample(total, out_ref):
    share = out_ref.shape[2]
    for i in range(out_ref.shape[0]):
        out_ref[i] = total[:, i * share : (i + 1) * share]


def first_sample_kernel(chunks, me_ref, slab_ref, cols_ref, probes_ref, out_ref, kept_ref, cols_out,
                        turned_out, probes_out, slab_ext, total):
    step = pl.program_id(0)
    width = cols_ref.shape[1]

    @pl.when(step == 0)
    def _():
        start_sample(chunks, me_ref, slab_ref, slab_ext, total)

    at = pl.ds(pl.multiple_of(step * width, width), width)
    cols = extended(cols_ref[...])
    probes = probes_ref[...]
    turned = cols.T
    cols_out[:, at] = cols
    turned_out[at, :] = turned
    probes_out[:, at] = probes
    mine = me_ref[1] * (kept_ref.shape[0] - 512)
    add_sample(slab_ext, turned, probes, total, kept_ref, step * width, mine)

    @pl.when(step == pl.num_programs(0) - 1)
    def _():
        end_sample(total, out_ref)


def next_sample_kernel(chunks, me_ref, slab_ref, cols_ref, probes_ref, _, out_ref, kept_ref, slab_ext,
                       total):
    start_sample(chunks, me_ref, slab_ref, slab_ext, total)
    width = 8192
    mine = me_ref[1] * (kept_ref.shape[0] - 512)

    @pl.loop(0, cols_ref.shape[0] // width)
    def _(step):
        at = pl.ds(pl.multiple_of(step * width, width), width)
        add_sample(slab_ext, cols_ref[at, :], probes_ref[:, at], total, kept_ref, step * width, mine)

    end_sample(total, out_ref)


def sample_scratch(chunks, share, n):
    count = len(chunks) * share
    return [pltpu.VMEM((128, count), jnp.bfloat16), pltpu.VMEM((n, count), jnp.float32)]


def sample_cost(count, points):
    return pl.CostEstimate(
        flops=4 * 256 * count * points, bytes_accessed=512 * points, transcendentals=count * points
    )


def first_sample_call(chunks, me, slab, cols, probes, own):
    _, dims, share = slab.shape
    n, points = probes.shape
    width = 4096
    return pl.pallas_call(
        functools.partial(first_sample_kernel, chunks),
        grid=(points // width,),
        in_specs=[
            SCALAR,
            WHOLE,
            pl.BlockSpec((dims, width), lambda i: (0, i)),
            pl.BlockSpec((n, width), lambda i: (0, i)),
        ],
        out_specs=[WHOLE] * 5,
        out_shape=[
            jax.ShapeDtypeStruct((len(chunks), n, share), jnp.float32),
            resident((own + 512, len(chunks) * share), jnp.bfloat16),
            resident((128, points), jnp.bfloat16),
            resident((points, 128), jnp.bfloat16),
            resident((n, points), jnp.bfloat16),
        ],
        scratch_shapes=sample_scratch(chunks, share, n),
        compiler_params=params(10),
        cost_estimate=sample_cost(len(chunks) * share, points),
        name="sample_first",
    )(me, slab, pinned(cols), pinned(probes))


def next_sample_call(chunks, me, slab, cols_ext, probes, own, after):
    _, dims, share = slab.shape
    n, points = probes.shape
    return pl.pallas_call(
        functools.partial(next_sample_kernel, chunks),
        in_specs=[SCALAR] + [WHOLE] * 4,
        out_specs=[WHOLE] * 2,
        out_shape=[
            jax.ShapeDtypeStruct((len(chunks), n, share), jnp.float32),
            resident((own + 512, len(chunks) * share), jnp.bfloat16),
        ],
        scratch_shapes=sample_scratch(chunks, share, n),
        compiler_params=params(8),
        cost_estimate=sample_cost(len(chunks) * share, points),
        name="sample_next",
    )(me, slab, held(cols_ext), held(probes), after)


def tile_kernel(chunks, me_ref, slab_ref, cols_ref, out_ref, token_ref, slab_ext):
    token_ref[...] = jnp.zeros_like(token_ref)
    count, wide = out_ref.shape
    side = me_ref[0] & 1
    points = [slab_ref[base + 2 * k + (side ^ flip)] for base, k, flip in chunks]
    slab_ext[...] = extended(jnp.concatenate(points, axis=1), scale_of(slab_ref)).T
    mine = me_ref[1] * wide
    width = min(4096, wide)

    @pl.loop(0, wide // width)
    def _(step):
        for j in range(width // 512):
            to = pl.multiple_of(step * width + j * 512, 512)
            cols = cols_ref[:, pl.ds(pl.multiple_of(mine + to, 512), 512)]
            for i in range(count // 512):
                rows = slice(i * 512, (i + 1) * 512)
                x = jnp.dot(slab_ext[rows, :], cols, preferred_element_type=jnp.float32)
                out_ref[rows, pl.ds(to, 512)] = jnp.exp(x).astype(jnp.bfloat16)


def tile_call(me, slab, chunks, cols_ext, wide):
    dims, share = slab.shape[1:]
    count = len(chunks) * share
    return pl.pallas_call(
        functools.partial(tile_kernel, chunks),
        in_specs=[SCALAR, WHOLE, WHOLE],
        out_specs=[WHOLE, WHOLE],
        out_shape=[
            resident((count, wide), jnp.bfloat16),
            jax.ShapeDtypeStruct((8, 128), jnp.float32),
        ],
        scratch_shapes=[pltpu.VMEM((count, 128), jnp.bfloat16)],
        compiler_params=params(6 + count // 1024),
        cost_estimate=pl.CostEstimate(
            flops=2 * 256 * count * wide,
            bytes_accessed=2 * count * wide,
            transcendentals=count * wide,
        ),
        name="tile",
    )(me, slab, held(cols_ext))


def sum_kernel(a_ref, b_ref, *refs):
    refs[-1][...] = a_ref[...] + b_ref[...]


def sum_call(a, b, *after):
    return pl.pallas_call(
        sum_kernel,
        in_specs=[WHOLE] * (2 + len(after)),
        out_specs=WHOLE,
        out_shape=jax.ShapeDtypeStruct(a.shape, a.dtype),
        compiler_params=params(8),
        name="sum",
    )(a, b, *after)


def later_kernel(x_ref, _, out_ref):
    out_ref[...] = x_ref[...]


def later_call(x, after):
    return pl.pallas_call(
        later_kernel,
        in_specs=[WHOLE] * 2,
        out_specs=WHOLE,
        out_shape=jax.ShapeDtypeStruct(x.shape, x.dtype),
        compiler_params=params(8),
        name="later",
    )(x, after)


def join_kernel(a_ref, b_ref, *refs):
    out_ref = refs[-1]
    half = a_ref.shape[0]
    out_ref[:half] = a_ref[...]
    out_ref[half:] = b_ref[...]


def join_call(a, b, *after):
    return pl.pallas_call(
        join_kernel,
        in_specs=[WHOLE] * (2 + len(after)),
        out_specs=WHOLE,
        out_shape=jax.ShapeDtypeStruct((2 * a.shape[0],) + a.shape[1:], a.dtype),
        compiler_params=params(8),
        name="join",
    )(a, b, *after)


def inverse_factor(gram):
    n = gram.shape[0]
    depth = 4
    high = 8
    shape = (high, 2 * n)
    diagonal = lax.broadcasted_iota(jnp.int32, (n, n), 0) == lax.broadcasted_iota(jnp.int32, (n, n), 1)
    work = jnp.concatenate([gram, jnp.where(diagonal, 1.0, 0.0)], axis=1)
    blocks = [work[i : i + high, :] for i in range(0, n, high)]
    row = lax.broadcasted_iota(jnp.int32, shape, 0)

    def spread(x):
        return jnp.broadcast_to(x, shape)

    for first in range(0, n, depth):
        home, at = divmod(first, high)
        columns = [
            [spread(block[:, first + i : first + i + 1]) for i in range(depth)] for block in blocks[home:]
        ]
        lines = [spread(blocks[home][at + i : at + i + 1, :]) for i in range(depth)]
        entry = {
            (i, j): spread(columns[0][j][at + i : at + i + 1, :])
            for i in range(depth)
            for j in range(i + 1)
        }
        roots = []
        for j in range(depth):
            root = lax.rsqrt(entry[j, j])
            roots.append(root)
            inverse = root * root
            for i in range(j + 1, depth):
                factor = entry[i, j] * inverse
                for k in range(j + 1, i + 1):
                    entry[i, k] = entry[i, k] - factor * entry[k, j]
                lines[i] = lines[i] - factor * lines[j]
                for column in columns:
                    column[i] = column[i] - factor * column[j]
        scaled = [line * root for line, root in zip(lines, roots)]
        for b, column in enumerate(columns):
            block = blocks[home + b]
            update = (column[0] * roots[0]) * scaled[0]
            for i in range(1, depth):
                update = update + (column[i] * roots[i]) * scaled[i]
            if b:
                block = block - update
            else:
                block = jnp.where(row >= at + depth, block - update, block)
                for i in range(depth):
                    block = jnp.where(row == at + i, scaled[i], block)
            blocks[home + b] = block
        yield None
    yield jnp.concatenate(blocks, axis=0)[:, n:]


def sides(ref, turned):
    n, share = ref.shape[1:]
    for i, chunk in enumerate(chunks_of(ref)):
        turned[:, i * share : (i + 1) * share] = jnp.concatenate(split(chunk, 3), axis=0)
    pieces = turned[...]
    whole = lax.dot_general(
        pieces, pieces, (((1,), (1,)), ((), ())), preferred_element_type=jnp.float32
    )
    lines = whole[:n] + whole[n : 2 * n] + whole[2 * n :]
    return lines[:, :n] + lines[:, n : 2 * n] + lines[:, 2 * n :]


def product(turned, tiles, at, n, columns_first=False):
    first = 0
    lines = None
    for tile in tiles:
        last = first + tile.shape[1 if columns_first else 0]
        part = lax.dot_general(
            turned[: 2 * n, first:last],
            tile[at, :] if columns_first else tile[:, at],
            (((1,), (1 if columns_first else 0,)), ((), ())),
            preferred_element_type=jnp.float32,
        )
        lines = part if lines is None else lines + part
        first = last
    return lines[:n] + lines[n:]


def side_scratch(count, n):
    return [pltpu.VMEM((3 * n, count), jnp.bfloat16)]


def partial_kernel(columns_first, sample_ref, *refs):
    *tiles, gram_ref, raw_ref, turned = refs
    n = sample_ref.shape[1]
    gram_ref[...] = sides(sample_ref, turned)
    width = 512
    for i in range(raw_ref.shape[1] // width):
        at = slice(i * width, (i + 1) * width)
        raw_ref[:, at] = product(turned, tiles, at, n, columns_first)


def partial_call(sample, tiles, wide, columns_first=False):
    parts, n, share = sample.shape
    count = parts * share
    return pl.pallas_call(
        functools.partial(partial_kernel, columns_first),
        in_specs=[WHOLE] * (1 + len(tiles)),
        out_specs=[WHOLE, WHOLE],
        out_shape=[
            jax.ShapeDtypeStruct((n, n), jnp.float32),
            jax.ShapeDtypeStruct((n, wide), jnp.float32),
        ],
        scratch_shapes=side_scratch(count, n),
        compiler_params=params(6 + count // 1024),
        cost_estimate=pl.CostEstimate(
            flops=2 * 256 * count * wide, bytes_accessed=2 * count * wide, transcendentals=0
        ),
        name="partial",
    )(sample, *[held(tile) for tile in tiles])


def finish_kernel(total, points, me_ref, sample_ref, near_ref, gram_a, gram_b, raw_a, raw_b, c_ref, d_ref,
                  basis_ref, image_ref, turned, raw, left):
    n = sample_ref.shape[1]
    step = pl.program_id(0)
    half, wide = c_ref.shape

    @pl.when(step == 0)
    def _():
        gram = (sides(sample_ref, turned) + gram_a[...] + gram_b[...]) / total
        rounds = inverse_factor(gram)
        width = wide // 8
        for i in range(8):
            rows = slice(i * width, (i + 1) * width)
            for _ in range(n // 32):
                next(rounds)
            raw[:, rows] = product(turned, (c_ref, d_ref), rows, n) + (raw_a[:, rows] + raw_b[:, rows])
        inverse = next(rounds)
        while inverse is None:
            inverse = next(rounds)
        diagonal = (
            lax.broadcasted_iota(jnp.int32, (n, n), 0) == lax.broadcasted_iota(jnp.int32, (n, n), 1)
        )
        trace = jnp.sum(jnp.where(diagonal, gram, 0.0), keepdims=True)
        scale = jnp.sqrt(float(n * points) / trace) / total
        basis_ref[...] = jnp.dot(
            inverse,
            near_ref[me_ref[0] // 2],
            precision=lax.Precision.HIGHEST,
            preferred_element_type=jnp.float32,
        ).astype(jnp.bfloat16)
        high, low = split(inverse * scale, 2)
        left[...] = jnp.concatenate([high, high, low, low], axis=1)

    @pl.when(step > 0)
    def _():
        width = image_ref.shape[1]
        at = pl.ds(pl.multiple_of((step - 1) * width, width), width)
        pieces = split(raw[:, at], 2)
        image_ref[...] = jnp.dot(
            left[...], jnp.concatenate(pieces + pieces, axis=0), preferred_element_type=jnp.float32
        )


def finish_call(me, sample, near, grams, raws, tiles, total, points):
    _, n, share = sample.shape
    half, wide = tiles[0].shape
    count = 2 * half
    width = wide // 2
    return pl.pallas_call(
        functools.partial(finish_kernel, float(total), float(points)),
        grid=(3,),
        in_specs=[SCALAR] + [WHOLE] * 8,
        out_specs=[
            pl.BlockSpec((n, share), lambda i: (0, 0)),
            pl.BlockSpec((n, width), lambda i: (0, jnp.maximum(i - 1, 0))),
        ],
        out_shape=[
            jax.ShapeDtypeStruct((n, share), jnp.bfloat16),
            jax.ShapeDtypeStruct((n, wide), jnp.float32),
        ],
        scratch_shapes=side_scratch(count, n)
        + [pltpu.VMEM((n, wide), jnp.float32), pltpu.VMEM((n, 4 * n), jnp.bfloat16)],
        compiler_params=params(8 + count // 1024),
        cost_estimate=pl.CostEstimate(
            flops=2 * 256 * count * wide, bytes_accessed=2 * count * wide, transcendentals=0
        ),
        name="finish",
    )(me, sample, near, *grams, *raws, held(tiles[0]), held(tiles[1]))


def exchanged(x, axis, stride):
    return lax.ppermute(x, axis, [(i ^ stride, i) for i in range(lax.axis_size(axis))])


def halvings(size):
    while size > 1:
        size //= 2
        yield size


def body(slab_points, col_points, probes):
    cols = lax.axis_size("col")
    rows = lax.axis_size("row")
    total = slab_points.shape[1] * cols * rows
    points = col_points.shape[1] * cols
    me = jnp.stack([lax.axis_index("col"), lax.axis_index("row")]).astype(jnp.int32)

    copies = jnp.broadcast_to(slab_points[None], (cols,) + slab_points.shape)
    slab = lax.all_to_all(copies, "col", 0, 0)

    order = [(k, flip) for flip in (0, 1) for k in range(cols // 2)]

    count = cols // 2
    half = count // 2
    strides = [stride for stride in halvings(cols) if stride > 1]
    own = col_points.shape[1] // rows
    part, first_kept, *prepared = first_sample_call(
        [(k, 1) for k in range(count)], me, slab, col_points, probes, own
    )
    got = exchanged(part, "col", 1)
    low, low_kept = next_sample_call([(k, 0) for k in range(half)], me, slab, *prepared[1:], own, part)
    low = low + got[:half]
    made, high_kept = next_sample_call(
        [(k, 0) for k in range(half, count)], me, slab, *prepared[1:], own, low
    )
    high = made + got[half:]
    kept = [low_kept, high_kept, first_kept]

    slabs = [later_call(slab, made)]
    for stride in halvings(rows):
        joined = slabs[0] if len(slabs) == 1 else jnp.concatenate(slabs, axis=0)
        slabs = [joined, exchanged(joined, "row", stride)]
    near = slabs[0].shape[0] // 2
    tiles = []
    spans = [(slabs[0], near), (slabs[1], 0), (slabs[1], near)]
    if rows > 4:
        spans = [(slabs[0], 0)] + spans
    for source, first in spans:
        chunks = [(base, k, flip) for base in range(first, first + near, cols) for k, flip in order]
        tiles.append(tile_call(me, source, chunks, prepared[0], own))
    tokens = [token for _, token in tiles]
    tiles = [tile for tile, _ in tiles]
    if rows > 4:
        tokens = [tokens[-1]] * 4

    for stride in strides:
        low = low + exchanged(low, "col", stride)
    for i, stride in enumerate(strides):
        high = sum_call(high, exchanged(high, "col", stride), *(tokens[:1] if i == 1 else []))
    sample = join_call(low, high)
    sample = join_call(sample, exchanged(sample, "col", 1), tokens[1])
    own_row = sample
    pieces = [sample]
    grams = []
    raws = []
    for stride in halvings(rows):
        if len(pieces) == 1:
            pieces.append(exchanged(pieces[0], "row", stride))
            continue
        wait = ()
        if stride == 1:
            gram, raw = partial_call(pieces[0], kept if rows == 4 else tiles[:1], own, rows == 4)
            grams.append(gram)
            raws.append(raw)
            wait = (gram, tokens[2])
        joined = join_call(*pieces, *wait)
        last = pieces[1]
        pieces = [joined, exchanged(joined, "row", stride)]
    gram, raw = partial_call(last, tiles[-3:-2], own)
    return tuple(
        finish_call(me, pieces[1], own_row, grams + [gram], raws + [raw], tiles[-2:], total, points)
    )


def solution(mesh):
    return jax.shard_map(
        body,
        mesh=mesh,
        in_specs=(P(None, ("row", "col")), P(None, "col"), P(None, "col")),
        out_specs=(P(None, ("row", "col")), P(None, ("col", "row"))),
        check_vma=False,
    )
```

time: 268 us -> 69.5 us (0.26)
  waiting for transfers between devices: 113 us -> 9.54 us
  matrix products: 70.3 us -> 0 us
  Pallas kernels: 0 us -> 39.3 us
  blocking collectives: 38.4 us -> 0 us
  starting transfers between devices: 0.08 us -> 18 us
  other arithmetic: 17.2 us -> 0.14 us
  between operations: 14.9 us -> 0.8 us
  local copies, waits for them, and re-layouts: 8.42 us -> 1.39 us
  loops' own time: 5.54 us -> 0 us
    psum x1 -> x0, waiting for transfers between devices: 69.9 us -> none  [body(): sample = lax.psum(partial_value, 'col')]
    dot_general x17 -> x0, matrix products: 68.9 us -> none  [the longest x8 35.1 us: image_step(): block_out = jnp.dot(basis_full, kernel, preferred_element_type=jnp.float32)]
    reduce_scatter x1 -> x0, waiting for transfers between devices: 42.7 us -> none  [body(): lax.psum_scatter(terms, 'row', scatter_dimension=1, tiled=True)]
    pallas_call x0 -> x15, Pallas kernels: none -> 39.3 us  [the longest x1 10.5 us: first_sample_call(): pl.pallas_call(functools.partial(first_sample_kernel, chunks), grid=(poin...]
    all_gather x1 -> x0, blocking collectives: 28.1 us -> none  [body(): slab_whole = lax.all_gather(slab_points, 'col', axis=1, tiled=True)]
    another operation x5 -> x1, other arithmetic: 12.1 us -> 0.07 us  [body(): jnp.stack([lax.axis_index('col'), lax.axis_index('row')]).astype(jnp.int32)]
    ppermute x0 -> x10, starting transfers between devices: none -> 10.7 us  [exchanged(): lax.ppermute(x, axis, [(i ^ stride, i) for i in range(lax.axis_size(axis))])]
    psum x1 -> x0, blocking collectives: 10.3 us -> none  [body(): lax.psum(jnp.dot(sample, sample.T, precision=lax.Precision.HIGHEST), 'row')]
  transfers between devices with their start and end apart: 2 -> 11, of which waited for: 2 -> 4; matrix products, arithmetic and copies ran while one was open for 0% -> 0% of each run, Pallas kernels for 0% -> 33%
where the time goes in v1:
time: 69.5 us; the launch traced here: 69.1 us
  Pallas kernels  39.3 us (57%)
  starting transfers between devices  18 us (26%)
  waiting for transfers between devices  9.54 us (14%)
  local copies, waits for them, and re-layouts  1.39 us (2%)
  between operations  0.8 us (1%)
    ppermute x10, starting transfers between devices, exchanged(): lax.ppermute(x, axis, [(i ^ stride, i) for i in range(lax.axis_size(axis))])  10.7 us
    pallas_call x1, Pallas kernels, first_sample_call(): pl.pallas_call(functools.partial(first_sample_kernel, chunks), grid=(poin...  10.5 us
    pallas_call x2, Pallas kernels, next_sample_call(): pl.pallas_call(functools.partial(next_sample_kernel, chunks), in_specs=[S...  10.1 us
    pallas_call x3, Pallas kernels, tile_call(): pl.pallas_call(functools.partial(tile_kernel, chunks), in_specs=[SCALAR,...  8.82 us
    all_to_all x1, waiting for transfers between devices, body(): slab = lax.all_to_all(copies, 'col', 0, 0)  7.27 us
    all_to_all x1, starting transfers between devices, body(): slab = lax.all_to_all(copies, 'col', 0, 0)  7.25 us
    pallas_call x1, Pallas kernels, finish_call(): pl.pallas_call(functools.partial(finish_kernel, float(total), float(point...  5.92 us
    pallas_call x2, Pallas kernels, partial_call(): pl.pallas_call(functools.partial(partial_kernel, columns_first), in_specs...  3.91 us
  transfers between devices with their start and end apart: 11, of which 4 were waited for; matrix products, arithmetic and copies ran while one was open for 0% of the time, Pallas kernels for 33%

profile of v1, /device:TPU:0, one launch (start us, length us, event | category | flops | bytes accessed | tf_op | source)
XLA Modules:
  0.0 69.1 jit_solution(9826562271936966350)
XLA Ops:
  0.6 1.4 %broadcast_in_dim.2 = bf16[8,64,128]{2,1,0:T(8,128)(2,1)} broadcast(bf16[64,128]{1,0:T(8,128)(2,1)} %param.3), dimensions={1,2} | broadcast | bytes 147456 | tf_op jit(solution)/shard_map/broadcast_in_dim | solution.py:494
  2.0 7.3 %all-to-all-start = ((bf16[8,64,128]{2,1,0:T(8,128)(2,1)}), bf16[8,64,128]{2,1,0:T(8,128)(2,1)S(1)}, u32[]{:S(2)}, u32[]{:S(2)}) async-start(bf16[8,64,128]{2,1,0:T(8,128)(2,1)} %broadcast_in_dim.2), calls=%async_computation | async-start | bytes 262144 | tf_op jit(solution)/shard_map/all_to_all | solution.py:495
  9.3 0.1 pad_add_fusion.me_ref
  9.3 7.3 %all-to-all-done.slab_ref.x_ref = bf16[8,64,128]{2,1,0:T(8,128)(2,1)S(1)} async-done(((bf16[8,64,128]{2,1,0:T(8,128)(2,1)}), bf16[8,64,128]{2,1,0:T(8,128)(2,1)S(1)}, u32[]{:S(2)}, u32[]{:S(2)}) %all-to-all-start) | async-done | bytes 131104 | tf_op jit(solution)/shard_map/all_to_all | solution.py:495
  16.6 10.5 %sample_first.1 = (f32[4,64,128]{2,1,0:T(8,128)S(1)}, bf16[4608,512]{1,0:T(8,128)(2,1)S(1)}, bf16[128,16384]{1,0:T(8,128)(2,1)S(1)}, bf16[16384,128]{1,0:T(8,128)(2,1)S(1)}, bf16[64,16384]{1,0:T(8,128)(2,1)S(1)}) custom-call(s32[2]{0:T(128)S(1)} %pad_add_fusion.me_ref, bf16[8,64,128]{2,1,0:T(8,128)(2,1)S(1)} %all-to-all-done.slab_ref.x_ref, ...), custom_call_target="tpu_custom_call" | custom-call | flops 8589934592 | bytes 8388608 | tf_op jit(solution)/shard_map/sample_first/pallas_call | solution.py:160
  27.1 0.3 collective-permute-start
  27.4 4.9 %sample_next.2 = (f32[2,64,128]{2,1,0:T(8,128)S(1)}, bf16[4608,256]{1,0:T(8,128)(2,1)S(1)}) custom-call(s32[2]{0:T(128)S(1)} %pad_add_fusion.me_ref, bf16[8,64,128]{2,1,0:T(8,128)(2,1)S(1)} %all-to-all-done.slab_ref.x_ref, bf16[16384,128]{1,0:T(8,128)(2,1)S(1)} %get-tuple-element.21.cols_ref, bf16[64,16384]{1,0:T(8,128)(2,1)S(1)} %get-tuple-element.22.probes_ref, ...), custom_call_target="tpu_custom_call" | custom-call | flops 4294967296 | bytes 8388608 | tf_op jit(solution)/shard_map/sample_next/pallas_call | solution.py:187
  32.3 0.0 collective-permute-done
  32.3 0.5 collective-permute-start.1
  32.8 5.1 %sample_next.3 = (f32[2,64,128]{2,1,0:T(8,128)S(1)}, bf16[4608,256]{1,0:T(8,128)(2,1)S(1)}) custom-call(s32[2]{0:T(128)S(1)} %pad_add_fusion.me_ref, bf16[8,64,128]{2,1,0:T(8,128)(2,1)S(1)} %all-to-all-done.slab_ref.x_ref, bf16[16384,128]{1,0:T(8,128)(2,1)S(1)} %get-tuple-element.21.cols_ref, bf16[64,16384]{1,0:T(8,128)(2,1)S(1)} %get-tuple-element.22.probes_ref, ...), custom_call_target="tpu_custom_call" | custom-call | flops 4294967296 | bytes 8388608 | tf_op jit(solution)/shard_map/sample_next/pallas_call | solution.py:187
  37.9 1.6 %collective-permute-start.5 = (bf16[8,64,128]{2,1,0:T(8,128)(2,1)S(1)}, bf16[8,64,128]{2,1,0:T(8,128)(2,1)S(1)}, u32[]{:S(2)}, u32[]{:S(2)}) collective-permute-start(bf16[8,64,128]{2,1,0:T(8,128)(2,1)S(1)} %later.1), channel_id=1, source_target_pairs={{16,0},{24,8},{0,16},{8,24},{17,1},{25,9},{1,17},{9,25},{18,2},{26... | collective-permute-start | bytes 393224 | tf_op jit(solution)/shard_map/ppermute | solution.py:478
  39.5 2.6 %collective-permute-start.3 = (f32[2,64,128]{2,1,0:T(8,128)S(1)}, f32[2,64,128]{2,1,0:T(8,128)S(1)}, u32[]{:S(2)}, u32[]{:S(2)}) collective-permute-start(f32[2,64,128]{2,1,0:T(8,128)S(1)} %slice_add_fusion.a_ref), channel_id=1, source_target_pairs={{4,0},{5,1},{6,2},{7,3},{0,4},{1,5},{2,6},{3,7},{12,8},{13,9},{14,... | collective-permute-start | bytes 196616 | tf_op jit(solution)/shard_map/ppermute | solution.py:478
  42.1 0.0 collective-permute-done.1
  42.2 1.2 %collective-permute-start.2 = (f32[2,64,128]{2,1,0:T(8,128)S(1)}, f32[2,64,128]{2,1,0:T(8,128)S(1)}, u32[]{:S(2)}, u32[]{:S(2)}) collective-permute-start(f32[2,64,128]{2,1,0:T(8,128)S(1)} %add.13), channel_id=1, source_target_pairs={{2,0},{3,1},{0,2},{1,3},{6,4},{7,5},{4,6},{5,7},{10,8},{11,9},{8,1... | collective-permute-start | bytes 196616 | tf_op jit(solution)/shard_map/ppermute | solution.py:478
  43.3 0.0 collective-permute-done.5
  43.4 0.1 collective-permute-start.7
  43.4 1.3 %collective-permute-done.3.b_ref = f32[2,64,128]{2,1,0:T(8,128)S(1)} collective-permute-done((f32[2,64,128]{2,1,0:T(8,128)S(1)}, f32[2,64,128]{2,1,0:T(8,128)S(1)}, u32[]{:S(2)}, u32[]{:S(2)}) %collective-permute-start.3) | collective-permute-done | bytes 65568 | tf_op jit(solution)/shard_map/ppermute | solution.py:478
  44.8 1.7 %collective-permute-start.4 = (f32[2,64,128]{2,1,0:T(8,128)S(1)}, f32[2,64,128]{2,1,0:T(8,128)S(1)}, u32[]{:S(2)}, u32[]{:S(2)}) collective-permute-start(f32[2,64,128]{2,1,0:T(8,128)S(1)} %sum.2.a_ref), channel_id=1, source_target_pairs={{2,0},{3,1},{0,2},{1,3},{6,4},{7,5},{4,6},{5,7},{10,8},{11,9},{8,1... | collective-permute-start | bytes 196616 | tf_op jit(solution)/shard_map/ppermute | solution.py:478
  46.5 0.0 collective-permute-done.2
  46.5 2.9 %tile.3 = (bf16[1024,4096]{1,0:T(8,128)(2,1)S(1)}, f32[8,128]{1,0:T(8,128)S(1)}) custom-call(s32[2]{0:T(128)S(1)} %pad_add_fusion.me_ref, bf16[16,64,128]{2,1,0:T(8,128)(2,1)S(1)} %pad_maximum_fusion.slab_ref, bf16[128,16384]{1,0:T(8,128)(2,1)S(1)} %get-tuple-element.26.cols_ref), custom_call_target="tpu_custom_call" | custom-call | flops 2147483648 | bytes 8388608 | tf_op jit(solution)/shard_map/tile/pallas_call | solution.py:225
  49.4 0.0 collective-permute-done.4.b_ref
  49.5 2.2 %collective-permute-start.6 = (f32[4,64,128]{2,1,0:T(8,128)S(1)}, f32[4,64,128]{2,1,0:T(8,128)S(1)}, u32[]{:S(2)}, u32[]{:S(2)}) collective-permute-start(f32[4,64,128]{2,1,0:T(8,128)S(1)} %join.3.a_ref), channel_id=1, source_target_pairs={{1,0},{0,1},{3,2},{2,3},{5,4},{4,5},{7,6},{6,7},{9,8},{8,9},{11,10... | collective-permute-start | bytes 393224 | tf_op jit(solution)/shard_map/ppermute | solution.py:478
  51.7 0.0 collective-permute-done.7.slab_ref
  51.7 2.9 %tile.4 = (bf16[1024,4096]{1,0:T(8,128)(2,1)S(1)}, f32[8,128]{1,0:T(8,128)S(1)}) custom-call(s32[2]{0:T(128)S(1)} %pad_add_fusion.me_ref, bf16[16,64,128]{2,1,0:T(8,128)(2,1)S(1)} %collective-permute-done.7.slab_ref, bf16[128,16384]{1,0:T(8,128)(2,1)S(1)} %get-tuple-element.26.cols_ref), custom_call_target="tpu_custom_call" | custom-call | flops 2147483648 | bytes 8388608 | tf_op jit(solution)/shard_map/tile/pallas_call | solution.py:225
  54.7 0.0 collective-permute-done.6.b_ref
  54.7 0.6 collective-permute-start.8
  55.3 2.5 %partial.2 = (f32[64,64]{1,0:T(8,128)S(1)}, f32[64,4096]{1,0:T(8,128)S(1)}) custom-call(f32[8,64,128]{2,1,0:T(8,128)S(1)} %join.4.sample_ref.a_ref.near_ref, bf16[4608,256]{1,0:T(8,128)(2,1)S(1)} %get-tuple-element.29.refs_0_, bf16[4608,256]{1,0:T(8,128)(2,1)S(1)} %get-tuple-element.30.refs_1_, bf16[4608,512]{1,0:T(8,128)(2,1)S(1)} %get-tuple-element.31.refs_2_), custom_call_target="tpu_custom_call" | custom-call | flops 2147483648 | bytes 8388608 | tf_op jit(solution)/shard_map/partial/pallas_call | solution.py:390
  57.8 2.9 %tile.5 = (bf16[1024,4096]{1,0:T(8,128)(2,1)S(1)}, f32[8,128]{1,0:T(8,128)S(1)}) custom-call(s32[2]{0:T(128)S(1)} %pad_add_fusion.me_ref, bf16[16,64,128]{2,1,0:T(8,128)(2,1)S(1)} %collective-permute-done.7.slab_ref, bf16[128,16384]{1,0:T(8,128)(2,1)S(1)} %get-tuple-element.26.cols_ref), custom_call_target="tpu_custom_call" | custom-call | flops 2147483648 | bytes 8388608 | tf_op jit(solution)/shard_map/tile/pallas_call | solution.py:225
  60.7 0.4 collective-permute-done.8.b_ref.sample_ref
  61.2 0.1 collective-permute-start.9
  61.3 1.4 %partial.3 = (f32[64,64]{1,0:T(8,128)S(1)}, f32[64,4096]{1,0:T(8,128)S(1)}) custom-call(f32[8,64,128]{2,1,0:T(8,128)S(1)} %collective-permute-done.8.b_ref.sample_ref, bf16[1024,4096]{1,0:T(8,128)(2,1)S(1)} %get-tuple-element.34.refs_0_), custom_call_target="tpu_custom_call" | custom-call | flops 2147483648 | bytes 8388608 | tf_op jit(solution)/shard_map/partial/pallas_call | solution.py:390
  62.7 0.5 collective-permute-done.9.sample_ref
  63.2 5.9 %finish.1 = (bf16[64,128]{1,0:T(8,128)(2,1)}, f32[64,4096]{1,0:T(8,128)}) custom-call(s32[2]{0:T(128)S(1)} %pad_add_fusion.me_ref, f32[16,64,128]{2,1,0:T(8,128)S(1)} %collective-permute-done.9.sample_ref, f32[8,64,128]{2,1,0:T(8,128)S(1)} %join.4.sample_ref.a_ref.near_ref, f32[64,64]{1,0:T(8,128)S(1)} %get-tuple-element.32.refs_0_.gram_a, ...), custom_call_target="tpu_custom_call" | custom-call | flops 4294967296 | bytes 16777216 | tf_op jit(solution)/shard_map/finish/pallas_call | solution.py:455
  (11 shorter events, 0.2 us)
Async XLA Ops:
  2.0 14.6 %all-to-all-start = ((bf16[8,64,128]{2,1,0:T(8,128)(2,1)}), bf16[8,64,128]{2,1,0:T(8,128)(2,1)S(1)}, u32[]{:S(2)}, u32[]{:S(2)}) async-start(bf16[8,64,128]{2,1,0:T(8,128)(2,1)} %broadcast_in_dim.2), calls=%async_computation | async-start | bytes 262144 | tf_op jit(solution)/shard_map/all_to_all | solution.py:495
  27.1 5.2 %collective-permute-start = (f32[4,64,128]{2,1,0:T(8,128)S(1)}, f32[4,64,128]{2,1,0:T(8,128)S(1)}, u32[]{:S(2)}, u32[]{:S(2)}) collective-permute-start(f32[4,64,128]{2,1,0:T(8,128)S(1)} %get-tuple-element.23._), channel_id=1, source_target_pairs={{1,0},{0,1},{3,2},{2,3},{5,4},{4,5},{7,6},{6,7},{9,8},{8,9},{11,10... | collective-permute-start | bytes 393224 | tf_op jit(solution)/shard_map/ppermute | solution.py:478
  32.3 9.8 %collective-permute-start.1 = (f32[2,64,128]{2,1,0:T(8,128)S(1)}, f32[2,64,128]{2,1,0:T(8,128)S(1)}, u32[]{:S(2)}, u32[]{:S(2)}) collective-permute-start(f32[2,64,128]{2,1,0:T(8,128)S(1)} %slice_add_fusion.1._), channel_id=1, source_target_pairs={{4,0},{5,1},{6,2},{7,3},{0,4},{1,5},{2,6},{3,7},{12,8},{13,9},{14,... | collective-permute-start | bytes 196616 | tf_op jit(solution)/shard_map/ppermute | solution.py:478
  37.9 5.4 %collective-permute-start.5 = (bf16[8,64,128]{2,1,0:T(8,128)(2,1)S(1)}, bf16[8,64,128]{2,1,0:T(8,128)(2,1)S(1)}, u32[]{:S(2)}, u32[]{:S(2)}) collective-permute-start(bf16[8,64,128]{2,1,0:T(8,128)(2,1)S(1)} %later.1), channel_id=1, source_target_pairs={{16,0},{24,8},{0,16},{8,24},{17,1},{25,9},{1,17},{9,25},{18,2},{26... | collective-permute-start | bytes 393224 | tf_op jit(solution)/shard_map/ppermute | solution.py:478
  39.5 5.2 %collective-permute-start.3 = (f32[2,64,128]{2,1,0:T(8,128)S(1)}, f32[2,64,128]{2,1,0:T(8,128)S(1)}, u32[]{:S(2)}, u32[]{:S(2)}) collective-permute-start(f32[2,64,128]{2,1,0:T(8,128)S(1)} %slice_add_fusion.a_ref), channel_id=1, source_target_pairs={{4,0},{5,1},{6,2},{7,3},{0,4},{1,5},{2,6},{3,7},{12,8},{13,9},{14,... | collective-permute-start | bytes 196616 | tf_op jit(solution)/shard_map/ppermute | solution.py:478
  42.2 4.3 %collective-permute-start.2 = (f32[2,64,128]{2,1,0:T(8,128)S(1)}, f32[2,64,128]{2,1,0:T(8,128)S(1)}, u32[]{:S(2)}, u32[]{:S(2)}) collective-permute-start(f32[2,64,128]{2,1,0:T(8,128)S(1)} %add.13), channel_id=1, source_target_pairs={{2,0},{3,1},{0,2},{1,3},{6,4},{7,5},{4,6},{5,7},{10,8},{11,9},{8,1... | collective-permute-start | bytes 196616 | tf_op jit(solution)/shard_map/ppermute | solution.py:478
  43.4 8.4 %collective-permute-start.7 = (bf16[16,64,128]{2,1,0:T(8,128)(2,1)S(1)}, bf16[16,64,128]{2,1,0:T(8,128)(2,1)S(1)}, u32[]{:S(2)}, u32[]{:S(2)}) collective-permute-start(bf16[16,64,128]{2,1,0:T(8,128)(2,1)S(1)} %pad_maximum_fusion.slab_ref), channel_id=1, source_target_pairs={{8,0},{0,8},{24,16},{16,24},{9,1},{1,9},{25,17},{17,25},{10,2},{2,... | collective-permute-start | bytes 786440 | tf_op jit(solution)/shard_map/ppermute | solution.py:478
  44.8 4.7 %collective-permute-start.4 = (f32[2,64,128]{2,1,0:T(8,128)S(1)}, f32[2,64,128]{2,1,0:T(8,128)S(1)}, u32[]{:S(2)}, u32[]{:S(2)}) collective-permute-start(f32[2,64,128]{2,1,0:T(8,128)S(1)} %sum.2.a_ref), channel_id=1, source_target_pairs={{2,0},{3,1},{0,2},{1,3},{6,4},{7,5},{4,6},{5,7},{10,8},{11,9},{8,1... | collective-permute-start | bytes 196616 | tf_op jit(solution)/shard_map/ppermute | solution.py:478
  49.5 5.2 %collective-permute-start.6 = (f32[4,64,128]{2,1,0:T(8,128)S(1)}, f32[4,64,128]{2,1,0:T(8,128)S(1)}, u32[]{:S(2)}, u32[]{:S(2)}) collective-permute-start(f32[4,64,128]{2,1,0:T(8,128)S(1)} %join.3.a_ref), channel_id=1, source_target_pairs={{1,0},{0,1},{3,2},{2,3},{5,4},{4,5},{7,6},{6,7},{9,8},{8,9},{11,10... | collective-permute-start | bytes 393224 | tf_op jit(solution)/shard_map/ppermute | solution.py:478
  54.7 6.4 %collective-permute-start.8 = (f32[8,64,128]{2,1,0:T(8,128)S(1)}, f32[8,64,128]{2,1,0:T(8,128)S(1)}, u32[]{:S(2)}, u32[]{:S(2)}) collective-permute-start(f32[8,64,128]{2,1,0:T(8,128)S(1)} %join.4.sample_ref.a_ref.near_ref), channel_id=1, source_target_pairs={{16,0},{24,8},{0,16},{8,24},{17,1},{25,9},{1,17},{9,25},{18,2},{26... | collective-permute-start | bytes 786440 | tf_op jit(solution)/shard_map/ppermute | solution.py:478
  61.2 2.0 %collective-permute-start.9 = (f32[16,64,128]{2,1,0:T(8,128)S(1)}, f32[16,64,128]{2,1,0:T(8,128)S(1)}, u32[]{:S(2)}, u32[]{:S(2)}) collective-permute-start(f32[16,64,128]{2,1,0:T(8,128)S(1)} %join.5), channel_id=1, source_target_pairs={{8,0},{0,8},{24,16},{16,24},{9,1},{1,9},{25,17},{17,25},{10,2},{2,... | collective-permute-start | bytes 1572872 | tf_op jit(solution)/shard_map/ppermute | solution.py:478

commit v2 on v1

--- a/solution.py
+++ b/solution.py
@@ -61,21 +61,20 @@
 
 def add_sample(slab_ext, cols, probes, total, kept_ref, first, mine):
     step = min(256, total.shape[1])
-    group = 4096
-    size = 512
-    own = kept_ref.shape[0] - size
+    group = 2048
+    own = kept_ref.shape[0] - 256
     places = []
-    for j in range(cols.shape[0] // size):
-        place = first + j * size - mine
+    for j in range(cols.shape[0] // 256):
+        place = first + j * 256 - mine
         place = jnp.where((place >= 0) & (place < own), place, own)
-        places.append(pl.ds(pl.multiple_of(place, size), size))
+        places.append(pl.ds(pl.multiple_of(place, 256), 256))
     for i in range(total.shape[1] // step):
         at = slice(i * step, (i + 1) * step)
         slab = slab_ext[:, at]
         for g in range(cols.shape[0] // group):
             kernel = []
-            for j in range(g * group // size, (g + 1) * group // size):
-                rows = slice(j * size, (j + 1) * size)
+            for j in range(g * group // 256, (g + 1) * group // 256):
+                rows = slice(j * 256, (j + 1) * 256)
                 x = jnp.dot(cols[rows, :], slab, preferred_element_type=jnp.float32)
                 k = jnp.exp(x).astype(jnp.bfloat16)
                 kept_ref[places[j], at] = k
@@ -120,7 +119,7 @@
     cols_out[:, at] = cols
     turned_out[at, :] = turned
     probes_out[:, at] = probes
-    mine = me_ref[1] * (kept_ref.shape[0] - 512)
+    mine = me_ref[1] * (kept_ref.shape[0] - 256)
     add_sample(slab_ext, turned, probes, total, kept_ref, step * width, mine)
 
     @pl.when(step == pl.num_programs(0) - 1)
@@ -132,7 +131,7 @@
                        total):
     start_sample(chunks, me_ref, slab_ref, slab_ext, total)
     width = 8192
-    mine = me_ref[1] * (kept_ref.shape[0] - 512)
+    mine = me_ref[1] * (kept_ref.shape[0] - 256)
 
     @pl.loop(0, cols_ref.shape[0] // width)
     def _(step):
@@ -169,7 +168,7 @@
         out_specs=[WHOLE] * 5,
         out_shape=[
             jax.ShapeDtypeStruct((len(chunks), n, share), jnp.float32),
-            resident((own + 512, len(chunks) * share), jnp.bfloat16),
+            resident((own + 256, len(chunks) * share), jnp.bfloat16),
             resident((128, points), jnp.bfloat16),
             resident((points, 128), jnp.bfloat16),
             resident((n, points), jnp.bfloat16),
@@ -190,7 +189,7 @@
         out_specs=[WHOLE] * 2,
         out_shape=[
             jax.ShapeDtypeStruct((len(chunks), n, share), jnp.float32),
-            resident((own + 512, len(chunks) * share), jnp.bfloat16),
+            resident((own + 256, len(chunks) * share), jnp.bfloat16),
         ],
         scratch_shapes=sample_scratch(chunks, share, n),
         compiler_params=params(8),
@@ -210,13 +209,13 @@
 
     @pl.loop(0, wide // width)
     def _(step):
-        for j in range(width // 512):
-            to = pl.multiple_of(step * width + j * 512, 512)
-            cols = cols_ref[:, pl.ds(pl.multiple_of(mine + to, 512), 512)]
+        for j in range(width // 256):
+            to = pl.multiple_of(step * width + j * 256, 256)
+            cols = cols_ref[:, pl.ds(pl.multiple_of(mine + to, 256), 256)]
             for i in range(count // 512):
                 rows = slice(i * 512, (i + 1) * 512)
                 x = jnp.dot(slab_ext[rows, :], cols, preferred_element_type=jnp.float32)
-                out_ref[rows, pl.ds(to, 512)] = jnp.exp(x).astype(jnp.bfloat16)
+                out_ref[rows, pl.ds(to, 256)] = jnp.exp(x).astype(jnp.bfloat16)
 
 
 def tile_call(me, slab, chunks, cols_ext, wide):
@@ -291,7 +290,7 @@
 
 def inverse_factor(gram):
     n = gram.shape[0]
-    depth = 4
+    depth = 8
     high = 8
     shape = (high, 2 * n)
     diagonal = lax.broadcasted_iota(jnp.int32, (n, n), 0) == lax.broadcasted_iota(jnp.int32, (n, n), 1)
@@ -417,7 +416,7 @@
         width = wide // 8
         for i in range(8):
             rows = slice(i * width, (i + 1) * width)
-            for _ in range(n // 32):
+            for _ in range(n // 64):
                 next(rounds)
             raw[:, rows] = product(turned, (c_ref, d_ref), rows, n) + (raw_a[:, rows] + raw_b[:, rows])
         inverse = next(rounds)

time: 69.5 us -> 68.4 us (0.984)
  Pallas kernels: 39.3 us -> 38.3 us
where the time goes in v2:
time: 68.4 us; the launch traced here: 68 us
  Pallas kernels  38.3 us (56%)
  starting transfers between devices  17.9 us (26%)
  waiting for transfers between devices  9.54 us (14%)
  local copies, waits for them, and re-layouts  1.39 us (2%)
  between operations  0.8 us (1%)
    ppermute x10, starting transfers between devices, exchanged(): lax.ppermute(x, axis, [(i ^ stride, i) for i in range(lax.axis_size(axis))])  10.7 us
    pallas_call x1, Pallas kernels, first_sample_call(): pl.pallas_call(functools.partial(first_sample_kernel, chunks), grid=(poin...  10.2 us
    pallas_call x2, Pallas kernels, next_sample_call(): pl.pallas_call(functools.partial(next_sample_kernel, chunks), in_specs=[S...  9.75 us
    pallas_call x3, Pallas kernels, tile_call(): pl.pallas_call(functools.partial(tile_kernel, chunks), in_specs=[SCALAR,...  8.84 us
    all_to_all x1, waiting for transfers between devices, body(): slab = lax.all_to_all(copies, 'col', 0, 0)  7.27 us
    all_to_all x1, starting transfers between devices, body(): slab = lax.all_to_all(copies, 'col', 0, 0)  7.25 us
    pallas_call x1, Pallas kernels, finish_call(): pl.pallas_call(functools.partial(finish_kernel, float(total), float(point...  5.44 us
    pallas_call x2, Pallas kernels, partial_call(): pl.pallas_call(functools.partial(partial_kernel, columns_first), in_specs...  3.91 us
  transfers between devices with their start and end apart: 11, of which 4 were waited for; matrix products, arithmetic and copies ran while one was open for 0% of the time, Pallas kernels for 33%

profile of v2, /device:TPU:0, one launch (start us, length us, event | category | flops | bytes accessed | tf_op | source)
XLA Modules:
  0.0 68.0 jit_solution(16122737855619451493)
XLA Ops:
  0.6 1.4 %broadcast_in_dim.2 = bf16[8,64,128]{2,1,0:T(8,128)(2,1)} broadcast(bf16[64,128]{1,0:T(8,128)(2,1)} %param.3), dimensions={1,2} | broadcast | bytes 147456 | tf_op jit(solution)/shard_map/broadcast_in_dim | solution.py:493
  2.0 7.3 %all-to-all-start = ((bf16[8,64,128]{2,1,0:T(8,128)(2,1)}), bf16[8,64,128]{2,1,0:T(8,128)(2,1)S(1)}, u32[]{:S(2)}, u32[]{:S(2)}) async-start(bf16[8,64,128]{2,1,0:T(8,128)(2,1)} %broadcast_in_dim.2), calls=%async_computation | async-start | bytes 262144 | tf_op jit(solution)/shard_map/all_to_all | solution.py:494
  9.3 0.1 pad_add_fusion.me_ref
  9.3 7.3 %all-to-all-done.slab_ref.x_ref = bf16[8,64,128]{2,1,0:T(8,128)(2,1)S(1)} async-done(((bf16[8,64,128]{2,1,0:T(8,128)(2,1)}), bf16[8,64,128]{2,1,0:T(8,128)(2,1)S(1)}, u32[]{:S(2)}, u32[]{:S(2)}) %all-to-all-start) | async-done | bytes 131104 | tf_op jit(solution)/shard_map/all_to_all | solution.py:494
  16.6 10.2 %sample_first.1 = (f32[4,64,128]{2,1,0:T(8,128)S(1)}, bf16[4352,512]{1,0:T(8,128)(2,1)S(1)}, bf16[128,16384]{1,0:T(8,128)(2,1)S(1)}, bf16[16384,128]{1,0:T(8,128)(2,1)S(1)}, bf16[64,16384]{1,0:T(8,128)(2,1)S(1)}) custom-call(s32[2]{0:T(128)S(1)} %pad_add_fusion.me_ref, bf16[8,64,128]{2,1,0:T(8,128)(2,1)S(1)} %all-to-all-done.slab_ref.x_ref, ...), custom_call_target="tpu_custom_call" | custom-call | flops 8589934592 | bytes 8388608 | tf_op jit(solution)/shard_map/sample_first/pallas_call | solution.py:159
  26.8 0.3 collective-permute-start
  27.1 4.8 %sample_next.2 = (f32[2,64,128]{2,1,0:T(8,128)S(1)}, bf16[4352,256]{1,0:T(8,128)(2,1)S(1)}) custom-call(s32[2]{0:T(128)S(1)} %pad_add_fusion.me_ref, bf16[8,64,128]{2,1,0:T(8,128)(2,1)S(1)} %all-to-all-done.slab_ref.x_ref, bf16[16384,128]{1,0:T(8,128)(2,1)S(1)} %get-tuple-element.21.cols_ref, bf16[64,16384]{1,0:T(8,128)(2,1)S(1)} %get-tuple-element.22.probes_ref, ...), custom_call_target="tpu_custom_call" | custom-call | flops 4294967296 | bytes 8388608 | tf_op jit(solution)/shard_map/sample_next/pallas_call | solution.py:186
  31.9 0.0 collective-permute-done
  31.9 0.4 collective-permute-start.1
  32.4 5.0 %sample_next.3 = (f32[2,64,128]{2,1,0:T(8,128)S(1)}, bf16[4352,256]{1,0:T(8,128)(2,1)S(1)}) custom-call(s32[2]{0:T(128)S(1)} %pad_add_fusion.me_ref, bf16[8,64,128]{2,1,0:T(8,128)(2,1)S(1)} %all-to-all-done.slab_ref.x_ref, bf16[16384,128]{1,0:T(8,128)(2,1)S(1)} %get-tuple-element.21.cols_ref, bf16[64,16384]{1,0:T(8,128)(2,1)S(1)} %get-tuple-element.22.probes_ref, ...), custom_call_target="tpu_custom_call" | custom-call | flops 4294967296 | bytes 8388608 | tf_op jit(solution)/shard_map/sample_next/pallas_call | solution.py:186
  37.4 1.6 %collective-permute-start.5 = (bf16[8,64,128]{2,1,0:T(8,128)(2,1)S(1)}, bf16[8,64,128]{2,1,0:T(8,128)(2,1)S(1)}, u32[]{:S(2)}, u32[]{:S(2)}) collective-permute-start(bf16[8,64,128]{2,1,0:T(8,128)(2,1)S(1)} %later.1), channel_id=1, source_target_pairs={{16,0},{24,8},{0,16},{8,24},{17,1},{25,9},{1,17},{9,25},{18,2},{26... | collective-permute-start | bytes 393224 | tf_op jit(solution)/shard_map/ppermute | solution.py:477
  39.0 2.6 %collective-permute-start.3 = (f32[2,64,128]{2,1,0:T(8,128)S(1)}, f32[2,64,128]{2,1,0:T(8,128)S(1)}, u32[]{:S(2)}, u32[]{:S(2)}) collective-permute-start(f32[2,64,128]{2,1,0:T(8,128)S(1)} %slice_add_fusion.a_ref), channel_id=1, source_target_pairs={{4,0},{5,1},{6,2},{7,3},{0,4},{1,5},{2,6},{3,7},{12,8},{13,9},{14,... | collective-permute-start | bytes 196616 | tf_op jit(solution)/shard_map/ppermute | solution.py:477
  41.6 0.0 collective-permute-done.1
  41.6 1.2 %collective-permute-start.2 = (f32[2,64,128]{2,1,0:T(8,128)S(1)}, f32[2,64,128]{2,1,0:T(8,128)S(1)}, u32[]{:S(2)}, u32[]{:S(2)}) collective-permute-start(f32[2,64,128]{2,1,0:T(8,128)S(1)} %add.13), channel_id=1, source_target_pairs={{2,0},{3,1},{0,2},{1,3},{6,4},{7,5},{4,6},{5,7},{10,8},{11,9},{8,1... | collective-permute-start | bytes 196616 | tf_op jit(solution)/shard_map/ppermute | solution.py:477
  42.7 0.0 collective-permute-done.5
  42.8 0.1 collective-permute-start.7
  42.9 1.4 %collective-permute-done.3.b_ref = f32[2,64,128]{2,1,0:T(8,128)S(1)} collective-permute-done((f32[2,64,128]{2,1,0:T(8,128)S(1)}, f32[2,64,128]{2,1,0:T(8,128)S(1)}, u32[]{:S(2)}, u32[]{:S(2)}) %collective-permute-start.3) | collective-permute-done | bytes 65568 | tf_op jit(solution)/shard_map/ppermute | solution.py:477
  44.2 1.7 %collective-permute-start.4 = (f32[2,64,128]{2,1,0:T(8,128)S(1)}, f32[2,64,128]{2,1,0:T(8,128)S(1)}, u32[]{:S(2)}, u32[]{:S(2)}) collective-permute-start(f32[2,64,128]{2,1,0:T(8,128)S(1)} %sum.2.a_ref), channel_id=1, source_target_pairs={{2,0},{3,1},{0,2},{1,3},{6,4},{7,5},{4,6},{5,7},{10,8},{11,9},{8,1... | collective-permute-start | bytes 196616 | tf_op jit(solution)/shard_map/ppermute | solution.py:477
  45.9 0.0 collective-permute-done.2
  45.9 3.0 %tile.3 = (bf16[1024,4096]{1,0:T(8,128)(2,1)S(1)}, f32[8,128]{1,0:T(8,128)S(1)}) custom-call(s32[2]{0:T(128)S(1)} %pad_add_fusion.me_ref, bf16[16,64,128]{2,1,0:T(8,128)(2,1)S(1)} %pad_maximum_fusion.slab_ref, bf16[128,16384]{1,0:T(8,128)(2,1)S(1)} %get-tuple-element.26.cols_ref), custom_call_target="tpu_custom_call" | custom-call | flops 2147483648 | bytes 8388608 | tf_op jit(solution)/shard_map/tile/pallas_call | solution.py:224
  48.9 0.0 collective-permute-done.4.b_ref
  48.9 2.2 %collective-permute-start.6 = (f32[4,64,128]{2,1,0:T(8,128)S(1)}, f32[4,64,128]{2,1,0:T(8,128)S(1)}, u32[]{:S(2)}, u32[]{:S(2)}) collective-permute-start(f32[4,64,128]{2,1,0:T(8,128)S(1)} %join.3.a_ref), channel_id=1, source_target_pairs={{1,0},{0,1},{3,2},{2,3},{5,4},{4,5},{7,6},{6,7},{9,8},{8,9},{11,10... | collective-permute-start | bytes 393224 | tf_op jit(solution)/shard_map/ppermute | solution.py:477
  51.2 0.0 collective-permute-done.7.slab_ref
  51.2 2.9 %tile.4 = (bf16[1024,4096]{1,0:T(8,128)(2,1)S(1)}, f32[8,128]{1,0:T(8,128)S(1)}) custom-call(s32[2]{0:T(128)S(1)} %pad_add_fusion.me_ref, bf16[16,64,128]{2,1,0:T(8,128)(2,1)S(1)} %collective-permute-done.7.slab_ref, bf16[128,16384]{1,0:T(8,128)(2,1)S(1)} %get-tuple-element.26.cols_ref), custom_call_target="tpu_custom_call" | custom-call | flops 2147483648 | bytes 8388608 | tf_op jit(solution)/shard_map/tile/pallas_call | solution.py:224
  54.1 0.0 collective-permute-done.6.b_ref
  54.2 0.6 collective-permute-start.8
  54.7 2.5 %partial.2 = (f32[64,64]{1,0:T(8,128)S(1)}, f32[64,4096]{1,0:T(8,128)S(1)}) custom-call(f32[8,64,128]{2,1,0:T(8,128)S(1)} %join.4.sample_ref.a_ref.near_ref, bf16[4352,256]{1,0:T(8,128)(2,1)S(1)} %get-tuple-element.29.refs_0_, bf16[4352,256]{1,0:T(8,128)(2,1)S(1)} %get-tuple-element.30.refs_1_, bf16[4352,512]{1,0:T(8,128)(2,1)S(1)} %get-tuple-element.31.refs_2_), custom_call_target="tpu_custom_call" | custom-call | flops 2147483648 | bytes 8388608 | tf_op jit(solution)/shard_map/partial/pallas_call | solution.py:389
  57.2 2.9 %tile.5 = (bf16[1024,4096]{1,0:T(8,128)(2,1)S(1)}, f32[8,128]{1,0:T(8,128)S(1)}) custom-call(s32[2]{0:T(128)S(1)} %pad_add_fusion.me_ref, bf16[16,64,128]{2,1,0:T(8,128)(2,1)S(1)} %collective-permute-done.7.slab_ref, bf16[128,16384]{1,0:T(8,128)(2,1)S(1)} %get-tuple-element.26.cols_ref), custom_call_target="tpu_custom_call" | custom-call | flops 2147483648 | bytes 8388608 | tf_op jit(solution)/shard_map/tile/pallas_call | solution.py:224
  60.2 0.4 collective-permute-done.8.b_ref.sample_ref
  60.6 0.1 collective-permute-start.9
  60.7 1.4 %partial.3 = (f32[64,64]{1,0:T(8,128)S(1)}, f32[64,4096]{1,0:T(8,128)S(1)}) custom-call(f32[8,64,128]{2,1,0:T(8,128)S(1)} %collective-permute-done.8.b_ref.sample_ref, bf16[1024,4096]{1,0:T(8,128)(2,1)S(1)} %get-tuple-element.34.refs_0_), custom_call_target="tpu_custom_call" | custom-call | flops 2147483648 | bytes 8388608 | tf_op jit(solution)/shard_map/partial/pallas_call | solution.py:389
  62.2 0.5 collective-permute-done.9.sample_ref
  62.6 5.4 %finish.1 = (bf16[64,128]{1,0:T(8,128)(2,1)}, f32[64,4096]{1,0:T(8,128)}) custom-call(s32[2]{0:T(128)S(1)} %pad_add_fusion.me_ref, f32[16,64,128]{2,1,0:T(8,128)S(1)} %collective-permute-done.9.sample_ref, f32[8,64,128]{2,1,0:T(8,128)S(1)} %join.4.sample_ref.a_ref.near_ref, f32[64,64]{1,0:T(8,128)S(1)} %get-tuple-element.32.refs_0_.gram_a, ...), custom_call_target="tpu_custom_call" | custom-call | flops 4294967296 | bytes 16777216 | tf_op jit(solution)/shard_map/finish/pallas_call | solution.py:454
  (11 shorter events, 0.2 us)
Async XLA Ops:
  2.0 14.6 %all-to-all-start = ((bf16[8,64,128]{2,1,0:T(8,128)(2,1)}), bf16[8,64,128]{2,1,0:T(8,128)(2,1)S(1)}, u32[]{:S(2)}, u32[]{:S(2)}) async-start(bf16[8,64,128]{2,1,0:T(8,128)(2,1)} %broadcast_in_dim.2), calls=%async_computation | async-start | bytes 262144 | tf_op jit(solution)/shard_map/all_to_all | solution.py:494
  26.8 5.1 %collective-permute-start = (f32[4,64,128]{2,1,0:T(8,128)S(1)}, f32[4,64,128]{2,1,0:T(8,128)S(1)}, u32[]{:S(2)}, u32[]{:S(2)}) collective-permute-start(f32[4,64,128]{2,1,0:T(8,128)S(1)} %get-tuple-element.23._), channel_id=1, source_target_pairs={{1,0},{0,1},{3,2},{2,3},{5,4},{4,5},{7,6},{6,7},{9,8},{8,9},{11,10... | collective-permute-start | bytes 393224 | tf_op jit(solution)/shard_map/ppermute | solution.py:477
  31.9 9.6 %collective-permute-start.1 = (f32[2,64,128]{2,1,0:T(8,128)S(1)}, f32[2,64,128]{2,1,0:T(8,128)S(1)}, u32[]{:S(2)}, u32[]{:S(2)}) collective-permute-start(f32[2,64,128]{2,1,0:T(8,128)S(1)} %slice_add_fusion.1._), channel_id=1, source_target_pairs={{4,0},{5,1},{6,2},{7,3},{0,4},{1,5},{2,6},{3,7},{12,8},{13,9},{14,... | collective-permute-start | bytes 196616 | tf_op jit(solution)/shard_map/ppermute | solution.py:477
  37.4 5.4 %collective-permute-start.5 = (bf16[8,64,128]{2,1,0:T(8,128)(2,1)S(1)}, bf16[8,64,128]{2,1,0:T(8,128)(2,1)S(1)}, u32[]{:S(2)}, u32[]{:S(2)}) collective-permute-start(bf16[8,64,128]{2,1,0:T(8,128)(2,1)S(1)} %later.1), channel_id=1, source_target_pairs={{16,0},{24,8},{0,16},{8,24},{17,1},{25,9},{1,17},{9,25},{18,2},{26... | collective-permute-start | bytes 393224 | tf_op jit(solution)/shard_map/ppermute | solution.py:477
  39.0 5.2 %collective-permute-start.3 = (f32[2,64,128]{2,1,0:T(8,128)S(1)}, f32[2,64,128]{2,1,0:T(8,128)S(1)}, u32[]{:S(2)}, u32[]{:S(2)}) collective-permute-start(f32[2,64,128]{2,1,0:T(8,128)S(1)} %slice_add_fusion.a_ref), channel_id=1, source_target_pairs={{4,0},{5,1},{6,2},{7,3},{0,4},{1,5},{2,6},{3,7},{12,8},{13,9},{14,... | collective-permute-start | bytes 196616 | tf_op jit(solution)/shard_map/ppermute | solution.py:477
  41.6 4.3 %collective-permute-start.2 = (f32[2,64,128]{2,1,0:T(8,128)S(1)}, f32[2,64,128]{2,1,0:T(8,128)S(1)}, u32[]{:S(2)}, u32[]{:S(2)}) collective-permute-start(f32[2,64,128]{2,1,0:T(8,128)S(1)} %add.13), channel_id=1, source_target_pairs={{2,0},{3,1},{0,2},{1,3},{6,4},{7,5},{4,6},{5,7},{10,8},{11,9},{8,1... | collective-permute-start | bytes 196616 | tf_op jit(solution)/shard_map/ppermute | solution.py:477
  42.8 8.4 %collective-permute-start.7 = (bf16[16,64,128]{2,1,0:T(8,128)(2,1)S(1)}, bf16[16,64,128]{2,1,0:T(8,128)(2,1)S(1)}, u32[]{:S(2)}, u32[]{:S(2)}) collective-permute-start(bf16[16,64,128]{2,1,0:T(8,128)(2,1)S(1)} %pad_maximum_fusion.slab_ref), channel_id=1, source_target_pairs={{8,0},{0,8},{24,16},{16,24},{9,1},{1,9},{25,17},{17,25},{10,2},{2,... | collective-permute-start | bytes 786440 | tf_op jit(solution)/shard_map/ppermute | solution.py:477
  44.2 4.7 %collective-permute-start.4 = (f32[2,64,128]{2,1,0:T(8,128)S(1)}, f32[2,64,128]{2,1,0:T(8,128)S(1)}, u32[]{:S(2)}, u32[]{:S(2)}) collective-permute-start(f32[2,64,128]{2,1,0:T(8,128)S(1)} %sum.2.a_ref), channel_id=1, source_target_pairs={{2,0},{3,1},{0,2},{1,3},{6,4},{7,5},{4,6},{5,7},{10,8},{11,9},{8,1... | collective-permute-start | bytes 196616 | tf_op jit(solution)/shard_map/ppermute | solution.py:477
  48.9 5.2 %collective-permute-start.6 = (f32[4,64,128]{2,1,0:T(8,128)S(1)}, f32[4,64,128]{2,1,0:T(8,128)S(1)}, u32[]{:S(2)}, u32[]{:S(2)}) collective-permute-start(f32[4,64,128]{2,1,0:T(8,128)S(1)} %join.3.a_ref), channel_id=1, source_target_pairs={{1,0},{0,1},{3,2},{2,3},{5,4},{4,5},{7,6},{6,7},{9,8},{8,9},{11,10... | collective-permute-start | bytes 393224 | tf_op jit(solution)/shard_map/ppermute | solution.py:477
  54.2 6.4 %collective-permute-start.8 = (f32[8,64,128]{2,1,0:T(8,128)S(1)}, f32[8,64,128]{2,1,0:T(8,128)S(1)}, u32[]{:S(2)}, u32[]{:S(2)}) collective-permute-start(f32[8,64,128]{2,1,0:T(8,128)S(1)} %join.4.sample_ref.a_ref.near_ref), channel_id=1, source_target_pairs={{16,0},{24,8},{0,16},{8,24},{17,1},{25,9},{1,17},{9,25},{18,2},{26... | collective-permute-start | bytes 786440 | tf_op jit(solution)/shard_map/ppermute | solution.py:477
  60.6 2.0 %collective-permute-start.9 = (f32[16,64,128]{2,1,0:T(8,128)S(1)}, f32[16,64,128]{2,1,0:T(8,128)S(1)}, u32[]{:S(2)}, u32[]{:S(2)}) collective-permute-start(f32[16,64,128]{2,1,0:T(8,128)S(1)} %join.5), channel_id=1, source_target_pairs={{8,0},{0,8},{24,16},{16,24},{9,1},{1,9},{25,17},{17,25},{10,2},{2,... | collective-permute-start | bytes 1572872 | tf_op jit(solution)/shard_map/ppermute | solution.py:477

commit v3 on v2

--- a/solution.py
+++ b/solution.py
@@ -416,7 +416,8 @@
         width = wide // 8
         for i in range(8):
             rows = slice(i * width, (i + 1) * width)
-            for _ in range(n // 64):
+            if i < 4:
+                next(rounds)
                 next(rounds)
             raw[:, rows] = product(turned, (c_ref, d_ref), rows, n) + (raw_a[:, rows] + raw_b[:, rows])
         inverse = next(rounds)
@@ -450,10 +451,10 @@
     _, n, share = sample.shape
     half, wide = tiles[0].shape
     count = 2 * half
-    width = wide // 2
+    width = wide
     return pl.pallas_call(
         functools.partial(finish_kernel, float(total), float(points)),
-        grid=(3,),
+        grid=(2,),
         in_specs=[SCALAR] + [WHOLE] * 8,
         out_specs=[
             pl.BlockSpec((n, share), lambda i: (0, 0)),
@@ -465,7 +466,7 @@
         ],
         scratch_shapes=side_scratch(count, n)
         + [pltpu.VMEM((n, wide), jnp.float32), pltpu.VMEM((n, 4 * n), jnp.bfloat16)],
-        compiler_params=params(8 + count // 1024),
+        compiler_params=params(10 + count // 1024),
         cost_estimate=pl.CostEstimate(
             flops=2 * 256 * count * wide, bytes_accessed=2 * count * wide, transcendentals=0
         ),

time: 68.4 us -> 68.4 us (level)
  no operation moved by 1% of the time
where the time goes in v3:
time: 68.4 us; the launch traced here: 68.1 us
  Pallas kernels  38.3 us (56%)
  starting transfers between devices  17.9 us (26%)
  waiting for transfers between devices  9.53 us (14%)
  local copies, waits for them, and re-layouts  1.39 us (2%)
  between operations  0.8 us (1%)
    ppermute x10, starting transfers between devices, exchanged(): lax.ppermute(x, axis, [(i ^ stride, i) for i in range(lax.axis_size(axis))])  10.7 us
    pallas_call x1, Pallas kernels, first_sample_call(): pl.pallas_call(functools.partial(first_sample_kernel, chunks), grid=(poin...  10.2 us
    pallas_call x2, Pallas kernels, next_sample_call(): pl.pallas_call(functools.partial(next_sample_kernel, chunks), in_specs=[S...  9.74 us
    pallas_call x3, Pallas kernels, tile_call(): pl.pallas_call(functools.partial(tile_kernel, chunks), in_specs=[SCALAR,...  8.84 us
    all_to_all x1, waiting for transfers between devices, body(): slab = lax.all_to_all(copies, 'col', 0, 0)  7.27 us
    all_to_all x1, starting transfers between devices, body(): slab = lax.all_to_all(copies, 'col', 0, 0)  7.25 us
    pallas_call x1, Pallas kernels, finish_call(): pl.pallas_call(functools.partial(finish_kernel, float(total), float(point...  5.46 us
    pallas_call x2, Pallas kernels, partial_call(): pl.pallas_call(functools.partial(partial_kernel, columns_first), in_specs...  3.91 us
  transfers between devices with their start and end apart: 11, of which 4 were waited for; matrix products, arithmetic and copies ran while one was open for 0% of the time, Pallas kernels for 33%

profile of v3, /device:TPU:0, one launch (start us, length us, event | category | flops | bytes accessed | tf_op | source)
XLA Modules:
  0.0 68.1 jit_solution(16025998051114600788)
XLA Ops:
  0.6 1.4 %broadcast_in_dim.2 = bf16[8,64,128]{2,1,0:T(8,128)(2,1)} broadcast(bf16[64,128]{1,0:T(8,128)(2,1)} %param.3), dimensions={1,2} | broadcast | bytes 147456 | tf_op jit(solution)/shard_map/broadcast_in_dim | solution.py:494
  2.0 7.3 %all-to-all-start = ((bf16[8,64,128]{2,1,0:T(8,128)(2,1)}), bf16[8,64,128]{2,1,0:T(8,128)(2,1)S(1)}, u32[]{:S(2)}, u32[]{:S(2)}) async-start(bf16[8,64,128]{2,1,0:T(8,128)(2,1)} %broadcast_in_dim.2), calls=%async_computation | async-start | bytes 262144 | tf_op jit(solution)/shard_map/all_to_all | solution.py:495
  9.3 0.1 pad_add_fusion.me_ref
  9.3 7.3 %all-to-all-done.slab_ref.x_ref = bf16[8,64,128]{2,1,0:T(8,128)(2,1)S(1)} async-done(((bf16[8,64,128]{2,1,0:T(8,128)(2,1)}), bf16[8,64,128]{2,1,0:T(8,128)(2,1)S(1)}, u32[]{:S(2)}, u32[]{:S(2)}) %all-to-all-start) | async-done | bytes 131104 | tf_op jit(solution)/shard_map/all_to_all | solution.py:495
  16.6 10.2 %sample_first.1 = (f32[4,64,128]{2,1,0:T(8,128)S(1)}, bf16[4352,512]{1,0:T(8,128)(2,1)S(1)}, bf16[128,16384]{1,0:T(8,128)(2,1)S(1)}, bf16[16384,128]{1,0:T(8,128)(2,1)S(1)}, bf16[64,16384]{1,0:T(8,128)(2,1)S(1)}) custom-call(s32[2]{0:T(128)S(1)} %pad_add_fusion.me_ref, bf16[8,64,128]{2,1,0:T(8,128)(2,1)S(1)} %all-to-all-done.slab_ref.x_ref, ...), custom_call_target="tpu_custom_call" | custom-call | flops 8589934592 | bytes 8388608 | tf_op jit(solution)/shard_map/sample_first/pallas_call | solution.py:159
  26.8 0.3 collective-permute-start
  27.1 4.8 %sample_next.2 = (f32[2,64,128]{2,1,0:T(8,128)S(1)}, bf16[4352,256]{1,0:T(8,128)(2,1)S(1)}) custom-call(s32[2]{0:T(128)S(1)} %pad_add_fusion.me_ref, bf16[8,64,128]{2,1,0:T(8,128)(2,1)S(1)} %all-to-all-done.slab_ref.x_ref, bf16[16384,128]{1,0:T(8,128)(2,1)S(1)} %get-tuple-element.21.cols_ref, bf16[64,16384]{1,0:T(8,128)(2,1)S(1)} %get-tuple-element.22.probes_ref, ...), custom_call_target="tpu_custom_call" | custom-call | flops 4294967296 | bytes 8388608 | tf_op jit(solution)/shard_map/sample_next/pallas_call | solution.py:186
  31.9 0.0 collective-permute-done
  31.9 0.5 collective-permute-start.1
  32.4 5.0 %sample_next.3 = (f32[2,64,128]{2,1,0:T(8,128)S(1)}, bf16[4352,256]{1,0:T(8,128)(2,1)S(1)}) custom-call(s32[2]{0:T(128)S(1)} %pad_add_fusion.me_ref, bf16[8,64,128]{2,1,0:T(8,128)(2,1)S(1)} %all-to-all-done.slab_ref.x_ref, bf16[16384,128]{1,0:T(8,128)(2,1)S(1)} %get-tuple-element.21.cols_ref, bf16[64,16384]{1,0:T(8,128)(2,1)S(1)} %get-tuple-element.22.probes_ref, ...), custom_call_target="tpu_custom_call" | custom-call | flops 4294967296 | bytes 8388608 | tf_op jit(solution)/shard_map/sample_next/pallas_call | solution.py:186
  37.4 1.6 %collective-permute-start.5 = (bf16[8,64,128]{2,1,0:T(8,128)(2,1)S(1)}, bf16[8,64,128]{2,1,0:T(8,128)(2,1)S(1)}, u32[]{:S(2)}, u32[]{:S(2)}) collective-permute-start(bf16[8,64,128]{2,1,0:T(8,128)(2,1)S(1)} %later.1), channel_id=1, source_target_pairs={{16,0},{24,8},{0,16},{8,24},{17,1},{25,9},{1,17},{9,25},{18,2},{26... | collective-permute-start | bytes 393224 | tf_op jit(solution)/shard_map/ppermute | solution.py:478
  39.0 2.6 %collective-permute-start.3 = (f32[2,64,128]{2,1,0:T(8,128)S(1)}, f32[2,64,128]{2,1,0:T(8,128)S(1)}, u32[]{:S(2)}, u32[]{:S(2)}) collective-permute-start(f32[2,64,128]{2,1,0:T(8,128)S(1)} %slice_add_fusion.a_ref), channel_id=1, source_target_pairs={{4,0},{5,1},{6,2},{7,3},{0,4},{1,5},{2,6},{3,7},{12,8},{13,9},{14,... | collective-permute-start | bytes 196616 | tf_op jit(solution)/shard_map/ppermute | solution.py:478
  41.6 0.0 collective-permute-done.1
  41.6 1.2 %collective-permute-start.2 = (f32[2,64,128]{2,1,0:T(8,128)S(1)}, f32[2,64,128]{2,1,0:T(8,128)S(1)}, u32[]{:S(2)}, u32[]{:S(2)}) collective-permute-start(f32[2,64,128]{2,1,0:T(8,128)S(1)} %add.13), channel_id=1, source_target_pairs={{2,0},{3,1},{0,2},{1,3},{6,4},{7,5},{4,6},{5,7},{10,8},{11,9},{8,1... | collective-permute-start | bytes 196616 | tf_op jit(solution)/shard_map/ppermute | solution.py:478
  42.7 0.0 collective-permute-done.5
  42.8 0.1 collective-permute-start.7
  42.8 1.3 %collective-permute-done.3.b_ref = f32[2,64,128]{2,1,0:T(8,128)S(1)} collective-permute-done((f32[2,64,128]{2,1,0:T(8,128)S(1)}, f32[2,64,128]{2,1,0:T(8,128)S(1)}, u32[]{:S(2)}, u32[]{:S(2)}) %collective-permute-start.3) | collective-permute-done | bytes 65568 | tf_op jit(solution)/shard_map/ppermute | solution.py:478
  44.2 1.7 %collective-permute-start.4 = (f32[2,64,128]{2,1,0:T(8,128)S(1)}, f32[2,64,128]{2,1,0:T(8,128)S(1)}, u32[]{:S(2)}, u32[]{:S(2)}) collective-permute-start(f32[2,64,128]{2,1,0:T(8,128)S(1)} %sum.2.a_ref), channel_id=1, source_target_pairs={{2,0},{3,1},{0,2},{1,3},{6,4},{7,5},{4,6},{5,7},{10,8},{11,9},{8,1... | collective-permute-start | bytes 196616 | tf_op jit(solution)/shard_map/ppermute | solution.py:478
  45.9 0.0 collective-permute-done.2
  45.9 2.9 %tile.3 = (bf16[1024,4096]{1,0:T(8,128)(2,1)S(1)}, f32[8,128]{1,0:T(8,128)S(1)}) custom-call(s32[2]{0:T(128)S(1)} %pad_add_fusion.me_ref, bf16[16,64,128]{2,1,0:T(8,128)(2,1)S(1)} %pad_maximum_fusion.slab_ref, bf16[128,16384]{1,0:T(8,128)(2,1)S(1)} %get-tuple-element.26.cols_ref), custom_call_target="tpu_custom_call" | custom-call | flops 2147483648 | bytes 8388608 | tf_op jit(solution)/shard_map/tile/pallas_call | solution.py:224
  48.9 0.0 collective-permute-done.4.b_ref
  48.9 2.2 %collective-permute-start.6 = (f32[4,64,128]{2,1,0:T(8,128)S(1)}, f32[4,64,128]{2,1,0:T(8,128)S(1)}, u32[]{:S(2)}, u32[]{:S(2)}) collective-permute-start(f32[4,64,128]{2,1,0:T(8,128)S(1)} %join.3.a_ref), channel_id=1, source_target_pairs={{1,0},{0,1},{3,2},{2,3},{5,4},{4,5},{7,6},{6,7},{9,8},{8,9},{11,10... | collective-permute-start | bytes 393224 | tf_op jit(solution)/shard_map/ppermute | solution.py:478
  51.1 0.0 collective-permute-done.7.slab_ref
  51.1 2.9 %tile.4 = (bf16[1024,4096]{1,0:T(8,128)(2,1)S(1)}, f32[8,128]{1,0:T(8,128)S(1)}) custom-call(s32[2]{0:T(128)S(1)} %pad_add_fusion.me_ref, bf16[16,64,128]{2,1,0:T(8,128)(2,1)S(1)} %collective-permute-done.7.slab_ref, bf16[128,16384]{1,0:T(8,128)(2,1)S(1)} %get-tuple-element.26.cols_ref), custom_call_target="tpu_custom_call" | custom-call | flops 2147483648 | bytes 8388608 | tf_op jit(solution)/shard_map/tile/pallas_call | solution.py:224
  54.1 0.0 collective-permute-done.6.b_ref
  54.1 0.6 collective-permute-start.8
  54.7 2.5 %partial.2 = (f32[64,64]{1,0:T(8,128)S(1)}, f32[64,4096]{1,0:T(8,128)S(1)}) custom-call(f32[8,64,128]{2,1,0:T(8,128)S(1)} %join.4.sample_ref.a_ref.near_ref, bf16[4352,256]{1,0:T(8,128)(2,1)S(1)} %get-tuple-element.29.refs_0_, bf16[4352,256]{1,0:T(8,128)(2,1)S(1)} %get-tuple-element.30.refs_1_, bf16[4352,512]{1,0:T(8,128)(2,1)S(1)} %get-tuple-element.31.refs_2_), custom_call_target="tpu_custom_call" | custom-call | flops 2147483648 | bytes 8388608 | tf_op jit(solution)/shard_map/partial/pallas_call | solution.py:389
  57.2 2.9 %tile.5 = (bf16[1024,4096]{1,0:T(8,128)(2,1)S(1)}, f32[8,128]{1,0:T(8,128)S(1)}) custom-call(s32[2]{0:T(128)S(1)} %pad_add_fusion.me_ref, bf16[16,64,128]{2,1,0:T(8,128)(2,1)S(1)} %collective-permute-done.7.slab_ref, bf16[128,16384]{1,0:T(8,128)(2,1)S(1)} %get-tuple-element.26.cols_ref), custom_call_target="tpu_custom_call" | custom-call | flops 2147483648 | bytes 8388608 | tf_op jit(solution)/shard_map/tile/pallas_call | solution.py:224
  60.1 0.4 collective-permute-done.8.b_ref.sample_ref
  60.6 0.1 collective-permute-start.9
  60.7 1.4 %partial.3 = (f32[64,64]{1,0:T(8,128)S(1)}, f32[64,4096]{1,0:T(8,128)S(1)}) custom-call(f32[8,64,128]{2,1,0:T(8,128)S(1)} %collective-permute-done.8.b_ref.sample_ref, bf16[1024,4096]{1,0:T(8,128)(2,1)S(1)} %get-tuple-element.34.refs_0_), custom_call_target="tpu_custom_call" | custom-call | flops 2147483648 | bytes 8388608 | tf_op jit(solution)/shard_map/partial/pallas_call | solution.py:389
  62.1 0.5 collective-permute-done.9.sample_ref
  62.6 5.5 %finish.1 = (bf16[64,128]{1,0:T(8,128)(2,1)}, f32[64,4096]{1,0:T(8,128)}) custom-call(s32[2]{0:T(128)S(1)} %pad_add_fusion.me_ref, f32[16,64,128]{2,1,0:T(8,128)S(1)} %collective-permute-done.9.sample_ref, f32[8,64,128]{2,1,0:T(8,128)S(1)} %join.4.sample_ref.a_ref.near_ref, f32[64,64]{1,0:T(8,128)S(1)} %get-tuple-element.32.refs_0_.gram_a, ...), custom_call_target="tpu_custom_call" | custom-call | flops 4294967296 | bytes 16777216 | tf_op jit(solution)/shard_map/finish/pallas_call | solution.py:455
  (11 shorter events, 0.2 us)
Async XLA Ops:
  2.0 14.6 %all-to-all-start = ((bf16[8,64,128]{2,1,0:T(8,128)(2,1)}), bf16[8,64,128]{2,1,0:T(8,128)(2,1)S(1)}, u32[]{:S(2)}, u32[]{:S(2)}) async-start(bf16[8,64,128]{2,1,0:T(8,128)(2,1)} %broadcast_in_dim.2), calls=%async_computation | async-start | bytes 262144 | tf_op jit(solution)/shard_map/all_to_all | solution.py:495
  26.8 5.1 %collective-permute-start = (f32[4,64,128]{2,1,0:T(8,128)S(1)}, f32[4,64,128]{2,1,0:T(8,128)S(1)}, u32[]{:S(2)}, u32[]{:S(2)}) collective-permute-start(f32[4,64,128]{2,1,0:T(8,128)S(1)} %get-tuple-element.23._), channel_id=1, source_target_pairs={{1,0},{0,1},{3,2},{2,3},{5,4},{4,5},{7,6},{6,7},{9,8},{8,9},{11,10... | collective-permute-start | bytes 393224 | tf_op jit(solution)/shard_map/ppermute | solution.py:478
  31.9 9.6 %collective-permute-start.1 = (f32[2,64,128]{2,1,0:T(8,128)S(1)}, f32[2,64,128]{2,1,0:T(8,128)S(1)}, u32[]{:S(2)}, u32[]{:S(2)}) collective-permute-start(f32[2,64,128]{2,1,0:T(8,128)S(1)} %slice_add_fusion.1._), channel_id=1, source_target_pairs={{4,0},{5,1},{6,2},{7,3},{0,4},{1,5},{2,6},{3,7},{12,8},{13,9},{14,... | collective-permute-start | bytes 196616 | tf_op jit(solution)/shard_map/ppermute | solution.py:478
  37.4 5.4 %collective-permute-start.5 = (bf16[8,64,128]{2,1,0:T(8,128)(2,1)S(1)}, bf16[8,64,128]{2,1,0:T(8,128)(2,1)S(1)}, u32[]{:S(2)}, u32[]{:S(2)}) collective-permute-start(bf16[8,64,128]{2,1,0:T(8,128)(2,1)S(1)} %later.1), channel_id=1, source_target_pairs={{16,0},{24,8},{0,16},{8,24},{17,1},{25,9},{1,17},{9,25},{18,2},{26... | collective-permute-start | bytes 393224 | tf_op jit(solution)/shard_map/ppermute | solution.py:478
  39.0 5.2 %collective-permute-start.3 = (f32[2,64,128]{2,1,0:T(8,128)S(1)}, f32[2,64,128]{2,1,0:T(8,128)S(1)}, u32[]{:S(2)}, u32[]{:S(2)}) collective-permute-start(f32[2,64,128]{2,1,0:T(8,128)S(1)} %slice_add_fusion.a_ref), channel_id=1, source_target_pairs={{4,0},{5,1},{6,2},{7,3},{0,4},{1,5},{2,6},{3,7},{12,8},{13,9},{14,... | collective-permute-start | bytes 196616 | tf_op jit(solution)/shard_map/ppermute | solution.py:478
  41.6 4.3 %collective-permute-start.2 = (f32[2,64,128]{2,1,0:T(8,128)S(1)}, f32[2,64,128]{2,1,0:T(8,128)S(1)}, u32[]{:S(2)}, u32[]{:S(2)}) collective-permute-start(f32[2,64,128]{2,1,0:T(8,128)S(1)} %add.13), channel_id=1, source_target_pairs={{2,0},{3,1},{0,2},{1,3},{6,4},{7,5},{4,6},{5,7},{10,8},{11,9},{8,1... | collective-permute-start | bytes 196616 | tf_op jit(solution)/shard_map/ppermute | solution.py:478
  42.8 8.4 %collective-permute-start.7 = (bf16[16,64,128]{2,1,0:T(8,128)(2,1)S(1)}, bf16[16,64,128]{2,1,0:T(8,128)(2,1)S(1)}, u32[]{:S(2)}, u32[]{:S(2)}) collective-permute-start(bf16[16,64,128]{2,1,0:T(8,128)(2,1)S(1)} %pad_maximum_fusion.slab_ref), channel_id=1, source_target_pairs={{8,0},{0,8},{24,16},{16,24},{9,1},{1,9},{25,17},{17,25},{10,2},{2,... | collective-permute-start | bytes 786440 | tf_op jit(solution)/shard_map/ppermute | solution.py:478
  44.2 4.7 %collective-permute-start.4 = (f32[2,64,128]{2,1,0:T(8,128)S(1)}, f32[2,64,128]{2,1,0:T(8,128)S(1)}, u32[]{:S(2)}, u32[]{:S(2)}) collective-permute-start(f32[2,64,128]{2,1,0:T(8,128)S(1)} %sum.2.a_ref), channel_id=1, source_target_pairs={{2,0},{3,1},{0,2},{1,3},{6,4},{7,5},{4,6},{5,7},{10,8},{11,9},{8,1... | collective-permute-start | bytes 196616 | tf_op jit(solution)/shard_map/ppermute | solution.py:478
  48.9 5.2 %collective-permute-start.6 = (f32[4,64,128]{2,1,0:T(8,128)S(1)}, f32[4,64,128]{2,1,0:T(8,128)S(1)}, u32[]{:S(2)}, u32[]{:S(2)}) collective-permute-start(f32[4,64,128]{2,1,0:T(8,128)S(1)} %join.3.a_ref), channel_id=1, source_target_pairs={{1,0},{0,1},{3,2},{2,3},{5,4},{4,5},{7,6},{6,7},{9,8},{8,9},{11,10... | collective-permute-start | bytes 393224 | tf_op jit(solution)/shard_map/ppermute | solution.py:478
  54.1 6.4 %collective-permute-start.8 = (f32[8,64,128]{2,1,0:T(8,128)S(1)}, f32[8,64,128]{2,1,0:T(8,128)S(1)}, u32[]{:S(2)}, u32[]{:S(2)}) collective-permute-start(f32[8,64,128]{2,1,0:T(8,128)S(1)} %join.4.sample_ref.a_ref.near_ref), channel_id=1, source_target_pairs={{16,0},{24,8},{0,16},{8,24},{17,1},{25,9},{1,17},{9,25},{18,2},{26... | collective-permute-start | bytes 786440 | tf_op jit(solution)/shard_map/ppermute | solution.py:478
  60.6 2.0 %collective-permute-start.9 = (f32[16,64,128]{2,1,0:T(8,128)S(1)}, f32[16,64,128]{2,1,0:T(8,128)S(1)}, u32[]{:S(2)}, u32[]{:S(2)}) collective-permute-start(f32[16,64,128]{2,1,0:T(8,128)S(1)} %join.5), channel_id=1, source_target_pairs={{8,0},{0,8},{24,16},{16,24},{9,1},{1,9},{25,17},{17,25},{10,2},{2,... | collective-permute-start | bytes 1572872 | tf_op jit(solution)/shard_map/ppermute | solution.py:478
